TPU v7x, 128 devices: a whole 4x4x4 slice. The times are simulated.
128 devices in a mesh: dp: 8 (over y, core), ctx: 16 (over z, x).
Axes of the slice: x: 4, y: 4, z: 4, core: 2. Of those that a mesh axis runs over, the one named last changes fastest.
Arguments:
- queries: bfloat16 [8, 3072, 4096], P('dp', 'ctx'), may hold values from -32 to 32
- keys: bfloat16 [8, 3072, 1024], P('dp', 'ctx'), may hold values from -6 to 6
- values: bfloat16 [8, 3072, 1024], P('dp', 'ctx'), may hold values from -6 to 6
- segment_ids: int32 [8, 3072], P('dp', 'ctx'), may hold values from 0 to 5, never falling along the last dimension, each value on 1 to 1536 neighbouring positions
- ssd_input: float32 [8, 3072, 4096], P('dp', 'ctx'), may hold values from -6 to 6
- b_matrix: float32 [8, 3072, 1024], P('dp', 'ctx'), may hold values from -0.5 to 0.5
- c_matrix: float32 [8, 3072, 1024], P('dp', 'ctx'), may hold values from -0.5 to 0.5
- step_size: float32 [8, 64, 3072], P('dp', None, 'ctx'), may hold values from 0.5 to 5376
- decay_log: float32 [64], replicated
- skip_gain: float32 [64], replicated, may hold values from 0.1 to 1.9
- cotangent: float32 [8, 3072, 4096], P('dp', 'ctx'), may hold values from -6 to 6
Outputs:
- attention_out: bfloat16 [8, 3072, 4096], P('dp', 'ctx')
- mixer_out: bfloat16 [8, 3072, 4096], P('dp', 'ctx')
- decay_grad: float32 [64], replicated
All inputs are finite; a program needn't handle non-finite values.
Results may differ from a plain program's by a relative error of at most 0.009.
Values may be sent and summed in bfloat16 or wider, within the bound.
A program may use at most 256 MiB of HBM per device.

v0:
```python
import jax
import jax.numpy as jnp
from jax import lax
from jax.sharding import PartitionSpec as P

Q_HEADS = 32
KV_HEADS = 8
HEAD_WIDTH = 128
SSD_HEADS = 64
HEAD_P = 64
STATE = 128
GROUPS = 8


precise = lax.Precision.HIGHEST


def from_behind(block, axis, distance):
    devices = range(lax.axis_size(axis))
    route = [(i - distance, i) for i in devices if i - distance in devices]
    return lax.ppermute(block, axis, route)


def entering(array, axis, combine, identity):
    count, place = (lax.axis_size(axis), lax.axis_index(axis))
    everything = jax.tree.map(
        lambda part, kind: lax.all_gather(part.astype(kind), axis),
        array,
        jax.tree.map(lambda a: jnp.bfloat16 if a.dtype == jnp.float32 else a.dtype, array),
    )
    start = jax.tree.map(
        lambda part, zero: jnp.broadcast_to(jnp.asarray(zero, part.dtype), part.shape),
        array,
        identity,
    )

    def step(k, before):
        reached = k < place
        new = combine(
            before, jax.tree.map(lambda part, own: part[k].astype(own.dtype), everything, array)
        )
        return jax.tree.map(lambda a, b: jnp.where(reached, a, b), new, before)

    return lax.fori_loop(0, count, step, start)


def join_states(earlier, later):
    span_a, state_a, hat_a, last_a = earlier
    span_b, state_b, hat_b, last_b = later
    linked = jnp.logical_or(last_a == last_b, last_b < 0.0)
    multiplier = jnp.where(linked, jnp.exp(span_b), 0.0)[..., None, None]
    state = multiplier * state_a + state_b
    hat = multiplier * (hat_a + span_b[..., None, None] * state_a) + hat_b
    last = jnp.where(last_b < 0.0, last_a, last_b)
    return (span_a + span_b, state, hat, last)


def decay_parts(step_blk, decay_log, groups):
    heads, count = step_blk.shape
    logs = step_blk * (-jnp.exp(decay_log))[:, None]
    return jnp.cumsum(logs, axis=1).reshape(groups, heads // groups, count)


def local_part(input_blk, b_blk, c_blk, forgetting_accrued, segment, grad_blk):
    count = input_blk.shape[0]
    groups, per_group = (forgetting_accrued.shape[0], forgetting_accrued.shape[1])
    inputs4 = input_blk.reshape(count, groups, per_group, -1)
    grads4 = grad_blk.reshape(count, groups, per_group, -1)
    b_groups = b_blk.reshape(count, groups, -1)
    c_groups = c_blk.reshape(count, groups, -1)
    place = jnp.arange(count, dtype=jnp.int32)
    mask = (place[None, :] <= place[:, None]) & (segment[None, :] == segment[:, None])
    gap = jnp.where(
        mask, forgetting_accrued[:, :, :, None] - forgetting_accrued[:, :, None, :], 0.0
    )
    inner = jnp.einsum("tgn,sgn->gts", c_groups, b_groups, precision=precise)
    weight = jnp.where(mask, jnp.exp(gap), 0.0) * inner[:, None]
    near = jnp.einsum("ghts,sghp->tghp", weight, inputs4, precision=precise)
    pairs = jnp.einsum("tghp,sghp->ghts", grads4, inputs4, precision=precise)
    grad_near = jnp.sum(weight * gap * pairs, axis=(2, 3)).reshape(-1)
    tail = forgetting_accrued[:, :, -1:] - forgetting_accrued
    keep = segment == segment[-1]
    end_weight = jnp.where(keep[None, None, :], jnp.exp(tail), 0.0)
    state_own = jnp.einsum("sgn,ghs,sghp->ghnp", b_groups, end_weight, inputs4, precision=precise)
    hat_own = jnp.einsum(
        "sgn,ghs,sghp->ghnp", b_groups, end_weight * tail, inputs4, precision=precise
    )
    element = (forgetting_accrued[:, :, -1], state_own, hat_own, segment[-1].astype(jnp.float32))
    return (near.reshape(count, -1), grad_near, element)


def carried_part(c_blk, forgetting_accrued, segment, grad_blk, state_in, hat_in, last_in):
    count = c_blk.shape[0]
    groups, per_group = (forgetting_accrued.shape[0], forgetting_accrued.shape[1])
    c_groups = c_blk.reshape(count, groups, -1)
    grads4 = grad_blk.reshape(count, groups, per_group, -1)
    live = segment.astype(jnp.float32) == last_in
    scale = jnp.where(live[None, None, :], jnp.exp(forgetting_accrued), 0.0).transpose(2, 0, 1)[
        ..., None
    ]
    sum_t = forgetting_accrued.transpose(2, 0, 1)[..., None]
    starting_position = jnp.einsum("tgn,ghnp->tghp", c_groups, state_in, precision=precise)
    extra = jnp.einsum("tgn,ghnp->tghp", c_groups, hat_in, precision=precise)
    far = starting_position * scale
    grad_far = jnp.sum(grads4 * (extra + sum_t * starting_position) * scale, axis=(0, 3)).reshape(
        -1
    )
    return (far.reshape(count, -1), grad_far)


def attend_tile(
    carry, query_head_count, key_tile, value_tile, segment_q, segment_k, query_pos, key_pos, valid
):
    run_max, run_total, weighted = carry
    groups = query_head_count.shape[1]
    key_head_count = key_tile.reshape(key_tile.shape[0], groups, -1)
    value_head_count = value_tile.reshape(value_tile.shape[0], groups, -1)
    score_matrix = jnp.einsum(
        "fkhu,nku->khfn", query_head_count, key_head_count, preferred_element_type=jnp.float32
    ) * query_head_count.shape[-1] ** (-0.5)
    mask = (
        (key_pos[None, :] <= query_pos[:, None])
        & (segment_k[None, :] == segment_q[:, None])
        & valid
    )
    row_top = jnp.max(jnp.where(mask, score_matrix, -1e30), axis=-1)
    new_max = jnp.maximum(run_max, row_top)
    exponent_weight = jnp.where(mask, jnp.exp(score_matrix - new_max[..., None]), 0.0)
    multiplier = jnp.exp(run_max - new_max)
    new_total = run_total * multiplier + jnp.sum(exponent_weight, axis=-1)
    part = jnp.einsum(
        "kvuc,ckw->ukvw",
        exponent_weight.astype(jnp.bfloat16),
        value_head_count,
        preferred_element_type=jnp.float32,
    )
    weighted = weighted * multiplier.transpose(2, 0, 1)[..., None] + part
    return (new_max, new_total, weighted)


def on_device(
    queries,
    keys,
    values,
    segment_ids,
    ssd_input,
    b_matrix,
    c_matrix,
    step_size,
    decay_log,
    skip_gain,
    cotangent,
):
    count = queries.shape[1]
    repeat_count = Q_HEADS // KV_HEADS
    query_head_count = queries[0].reshape(count, KV_HEADS, repeat_count, HEAD_WIDTH)
    segment_row = segment_ids[0]
    position = lax.axis_index("ctx")
    query_pos = position * count + jnp.arange(count, dtype=jnp.int32)
    start_carry = (
        jnp.full((KV_HEADS, repeat_count, count), -1e30, jnp.float32),
        jnp.zeros((KV_HEADS, repeat_count, count), jnp.float32),
        jnp.zeros((count, KV_HEADS, repeat_count, HEAD_WIDTH), jnp.float32),
    )
    carry = attend_tile(
        start_carry,
        query_head_count,
        keys[0],
        values[0],
        segment_row,
        segment_row,
        query_pos,
        query_pos,
        True,
    )

    def turn_step(turn, state):
        carry_in, moving = state
        moving = from_behind((moving[0], moving[1], moving[2]), "ctx", 1)
        key_pos = query_pos - turn * count
        valid = position >= turn
        carry_out = attend_tile(
            carry_in,
            query_head_count,
            moving[0],
            moving[1],
            segment_row,
            moving[2],
            query_pos,
            key_pos,
            valid,
        )
        return (carry_out, moving)

    carry, moved = lax.fori_loop(
        1, lax.axis_size("ctx"), turn_step, (carry, (keys[0], values[0], segment_row))
    )
    run_max, run_total, weighted = carry
    attention_out = (
        (weighted / run_total.transpose(2, 0, 1)[..., None])
        .reshape(1, count, -1)
        .astype(jnp.bfloat16)
    )
    input_blk = ssd_input[0]
    grad_blk = cotangent[0]
    forgetting_accrued = decay_parts(step_size[0], decay_log, GROUPS)
    near, grad_near, element = local_part(
        input_blk, b_matrix[0], c_matrix[0], forgetting_accrued, segment_row, grad_blk
    )
    per_group = SSD_HEADS // GROUPS
    identity = (
        jnp.zeros((GROUPS, per_group), jnp.float32),
        jnp.zeros((GROUPS, per_group, STATE, HEAD_P), jnp.float32),
        jnp.zeros((GROUPS, per_group, STATE, HEAD_P), jnp.float32),
        jnp.array(-1.0, jnp.float32),
    )
    prefix = entering(element, "ctx", join_states, identity)
    far, grad_far = carried_part(
        c_matrix[0], forgetting_accrued, segment_row, grad_blk, prefix[1], prefix[2], prefix[3]
    )
    mixed = near + far + input_blk * jnp.repeat(skip_gain, HEAD_P)[None, :]
    grand = lax.psum(grad_near + grad_far, ("dp", "ctx"))
    decay_grad = grand / (lax.axis_size("dp") * lax.axis_size("ctx") * count)
    return (attention_out, mixed.astype(jnp.bfloat16).reshape(1, count, -1), decay_grad)


def solution(mesh):
    return jax.shard_map(
        on_device,
        mesh=mesh,
        in_specs=(
            P("dp", "ctx", None),
            P("dp", "ctx", None),
            P("dp", "ctx", None),
            P("dp", "ctx"),
            P("dp", "ctx", None),
            P("dp", "ctx", None),
            P("dp", "ctx", None),
            P("dp", None, "ctx"),
            P(),
            P(),
            P("dp", "ctx", None),
        ),
        out_specs=(P("dp", "ctx", None), P("dp", "ctx", None), P()),
        check_vma=False,
    )
```

profile of v0, /device:TPU:1, one launch (start us, length us, event | category | flops | bytes accessed | tf_op | source)
XLA Modules:
  0.0 1063.7 jit_solution(10628553868999065731)
XLA Ops:
  14.6 5.2 copy.137
  20.8 7.1 fusion.61
  28.0 7.1 fusion.58
  38.3 36.7 %all-reduce.1 = bf16[16]{0:T(256)(128)(2,1)} all-reduce(bf16[16]{0:T(256)(128)(2,1)S(1)} %dynamic-update-slice), channel_id=1, replica_groups=mesh['dp'=8,'ctx'=16] {'ctx'}, use_global_device_ids=true, to_apply=%add.1 | all-reduce | flops 16 | bytes 64
  76.1 5.3 copy.148
  95.1 522.7 %while.42 = (s32[]{:T(128)}, f32[8,4,192]{2,1,0:T(4,128)}, f32[8,4,192]{2,1,0:T(4,128)}, f32[192,8,4,128]{3,0,2,1:T(8,128)S(1)}, bf16[192,1024]{1,0:T(8,128)(2,1...) while((s32[]{:T(128)}, f32[8,4,192]{2,1,0:T(4,128)}, ...), condition=%wide.region_5.6_spmd.clone, body=%wide.region_2.5_spmd.clone.sunk | while | flops 618695040 | bytes 31516036 | solution.py:195
  100.7 28.4 %collective-permute-done = s32[192]{0:T(256)S(1)} collective-permute-done((s32[192]{0:T(256)}, s32[192]{0:T(256)S(1)}, u32[]{:S(2)}, u32[]{:S(2)}) %collective-permute-start) | collective-permute-done | bytes 800 | tf_op jit(solution)/shard_map/while/body/eval_jaxpr/ppermute | solution.py:21
  149.4 20.6 %collective-permute-done = s32[192]{0:T(256)S(1)} collective-permute-done((s32[192]{0:T(256)}, s32[192]{0:T(256)S(1)}, u32[]{:S(2)}, u32[]{:S(2)}) %collective-permute-start) | collective-permute-done | bytes 800 | tf_op jit(solution)/shard_map/while/body/eval_jaxpr/ppermute | solution.py:21
  193.0 26.1 %collective-permute-done = s32[192]{0:T(256)S(1)} collective-permute-done((s32[192]{0:T(256)}, s32[192]{0:T(256)S(1)}, u32[]{:S(2)}, u32[]{:S(2)}) %collective-permute-start) | collective-permute-done | bytes 800 | tf_op jit(solution)/shard_map/while/body/eval_jaxpr/ppermute | solution.py:21
  242.1 27.1 %collective-permute-done = s32[192]{0:T(256)S(1)} collective-permute-done((s32[192]{0:T(256)}, s32[192]{0:T(256)S(1)}, u32[]{:S(2)}, u32[]{:S(2)}) %collective-permute-start) | collective-permute-done | bytes 800 | tf_op jit(solution)/shard_map/while/body/eval_jaxpr/ppermute | solution.py:21
  292.9 26.1 %collective-permute-done = s32[192]{0:T(256)S(1)} collective-permute-done((s32[192]{0:T(256)}, s32[192]{0:T(256)S(1)}, u32[]{:S(2)}, u32[]{:S(2)}) %collective-permute-start) | collective-permute-done | bytes 800 | tf_op jit(solution)/shard_map/while/body/eval_jaxpr/ppermute | solution.py:21
  339.6 5.3 collective-permute-start
  361.2 5.2 collective-permute-start.1
  366.4 7.0 collective-permute-start.2
  377.2 4.7 collective-permute-done
  394.1 5.3 collective-permute-start.1
  399.4 6.2 collective-permute-start.2
  409.0 5.2 collective-permute-done
  426.3 4.9 collective-permute-start.1
  431.2 5.5 collective-permute-start.2
  440.1 5.0 collective-permute-done
  461.4 5.2 collective-permute-start.2
  591.5 5.6 collective-permute-start.1
  597.2 5.0 collective-permute-start.2
  623.2 26.5 %all-gather = bf16[128,8,1]{1,0,2:T(8,128)(2,1)S(1)} all-gather(bf16[8,8,1]{1,0,2:T(8,128)(2,1)S(1)} %copy-done.27), channel_id=2, replica_groups=mesh['dp'=8,'ctx'=16] {'ctx'}, dimensions={0}, use_global_device_ids=true | all-gather | bytes 2176 | tf_op jit(solution)/shard_map/all_gather | solution.py:27
  652.5 18.4 %multiply_reduce_fusion = f32[8,8]{1,0:T(8,128)S(1)} fusion(f32[8,192,192]{2,1,0:T(8,128)S(1)} %fusion.64, f32[8,8,192]{2,1,0:T(8,128)S(1)} %copy-done.23, pred[192,192]{1,0:T(8,128)(4,1)S(1)} %copy-done.26, f32[192,8,8,64]{0,3,2,1:T(8,128)} %bitcast.207, f32[192,8,8,64]{0,3,2,1:T(8,128)} %bitcast.204), kind=kOutput, calls=%fused_computation.33 | convolution fusion | flops 1828454400 | bytes 7557376 | tf_op jit(solution)/shard_map/tghp,sghp->ghts/dot_general | solution.py:79
  671.0 259.5 %while.43 = (s32[]{:T(128)}, f32[8,8,128,64]{3,2,1,0:T(8,128)}, f32[8,8,128,64]{3,2,1,0:T(8,128)}, f32[]{:T(128)}, s32[]{:T(128)}, /*index=5*/bf16[16]{0:T(256)(...) while((s32[]{:T(128)}, f32[8,8,128,64]{3,2,1,0:T(8,128)}, ...), condition=%wide.region_9.10_spmd.clone, body=%wide.region_8.9_spmd.clone.sunk | while | flops 6291657 | bytes 18875844 | solution.py:44
  679.5 5.6 fusion.101
  694.3 7.1 fusion.101
  710.6 7.1 fusion.101
  726.9 7.1 fusion.101
  743.2 7.1 fusion.101
  759.5 7.1 fusion.101
  775.9 7.1 fusion.101
  792.2 7.1 fusion.101
  808.6 7.1 fusion.101
  824.9 7.1 fusion.101
  841.2 7.1 fusion.101
  857.5 7.1 fusion.101
  873.8 7.1 fusion.101
  890.1 7.1 fusion.101
  906.4 7.1 fusion.101
  922.7 7.1 fusion.101
  930.6 9.3 fusion.68
  939.9 17.7 %fusion.37 = f32[192,8,8,64]{0,3,2,1:T(8,128)} fusion(f32[8,8,64,192]{3,2,1,0:T(8,128)S(1)} %fusion.68, f32[192,8,8,64]{0,3,2,1:T(8,128)S(1)} %bitcast.205, f32[8,192,192]{2,1,0:T(8,128)S(1)} %copy-done.14, f32[8,8,192]{2,1,0:T(8,128)S(1)} %copy-done.23, pred[192,192]{1,0:T(8,128)(4,1)S(1)} %copy-done.26, f32[192,8,8]{0,2,1:T(8,128)S(1)} %select_bitcast_fusion), kind=kOutput, calls=%fused_computation.55 | convolution fusion | flops 1822949376 | bytes 10752000 | tf_op jit(solution)/shard_map/ghts,sghp->tghp/dot_general | solution.py:78
  957.7 7.9 fusion.36
  965.7 81.4 %psum.7 = f32[64]{0:T(128)S(1)} all-reduce(f32[64]{0:T(128)S(1)} %add.134), channel_id=1, replica_groups=mesh['dp'=8,'ctx'=16] {'dp','ctx'}, use_global_device_ids=true, to_apply=%region_12.13 | all-reduce | flops 64 | bytes 512 | tf_op jit(solution)/shard_map/psum | solution.py:222
  1047.6 5.3 copy.147
  (592 shorter events, 475.1 us)
Async XLA Ops:
  7.2 663.8 %all-gather.6.cloned.1.call-start = ((), (), s32[]{:S(2)}) async-start(), calls=%async_computation | async-start | bytes 17825792 | tf_op jit(solution)/shard_map/all_gather | solution.py:27
  27.9 643.0 %all-gather.8.cloned.1.call-start = ((), (), s32[]{:S(2)}) async-start(), calls=%async_computation.1 | async-start | bytes 17825792 | tf_op jit(solution)/shard_map/all_gather | solution.py:27
  96.1 33.7 %collective-permute-start.1 = (bf16[192,1024]{1,0:T(8,128)(2,1)}, bf16[192,1024]{1,0:T(8,128)(2,1)S(1)}, u32[]{:S(2)}, u32[]{:S(2)}) collective-permute-start(bf16[192,1024]{1,0:T(8,128)(2,1)} %get-tuple-element.712), channel_id=1, source_target_pairs={{0,1},{1,2},{2,3},{3,4},{4,5},{5,6},{6,7},{7,8},{8,9},{9,10},{10,1... | collective-permute-start | bytes 1179656 | tf_op jit(solution)/shard_map/while/body/eval_jaxpr/ppermute | solution.py:21
  97.4 32.5 %collective-permute-start.2 = (bf16[192,1024]{1,0:T(8,128)(2,1)}, bf16[192,1024]{1,0:T(8,128)(2,1)}, u32[]{:S(2)}, u32[]{:S(2)}) collective-permute-start(bf16[192,1024]{1,0:T(8,128)(2,1)} %copy-done.15), channel_id=1, source_target_pairs={{0,1},{1,2},{2,3},{3,4},{4,5},{5,6},{6,7},{7,8},{8,9},{9,10},{10,1... | collective-permute-start | bytes 1179656 | tf_op jit(solution)/shard_map/while/body/eval_jaxpr/ppermute | solution.py:21
  99.4 29.7 %collective-permute-start = (s32[192]{0:T(256)}, s32[192]{0:T(256)S(1)}, u32[]{:S(2)}, u32[]{:S(2)}) collective-permute-start(s32[192]{0:T(256)} %get-tuple-element.714), channel_id=1, source_target_pairs={{0,1},{1,2},{2,3},{3,4},{4,5},{5,6},{6,7},{7,8},{8,9},{9,10},{10,1... | collective-permute-start | bytes 2312 | tf_op jit(solution)/shard_map/while/body/eval_jaxpr/ppermute | solution.py:21
  141.4 29.3 %collective-permute-start.1 = (bf16[192,1024]{1,0:T(8,128)(2,1)}, bf16[192,1024]{1,0:T(8,128)(2,1)S(1)}, u32[]{:S(2)}, u32[]{:S(2)}) collective-permute-start(bf16[192,1024]{1,0:T(8,128)(2,1)} %get-tuple-element.712), channel_id=1, source_target_pairs={{0,1},{1,2},{2,3},{3,4},{4,5},{5,6},{6,7},{7,8},{8,9},{9,10},{10,1... | collective-permute-start | bytes 1179656 | tf_op jit(solution)/shard_map/while/body/eval_jaxpr/ppermute | solution.py:21
  145.4 25.3 %collective-permute-start.2 = (bf16[192,1024]{1,0:T(8,128)(2,1)}, bf16[192,1024]{1,0:T(8,128)(2,1)}, u32[]{:S(2)}, u32[]{:S(2)}) collective-permute-start(bf16[192,1024]{1,0:T(8,128)(2,1)} %copy-done.15), channel_id=1, source_target_pairs={{0,1},{1,2},{2,3},{3,4},{4,5},{5,6},{6,7},{7,8},{8,9},{9,10},{10,1... | collective-permute-start | bytes 1179656 | tf_op jit(solution)/shard_map/while/body/eval_jaxpr/ppermute | solution.py:21
  148.1 21.9 %collective-permute-start = (s32[192]{0:T(256)}, s32[192]{0:T(256)S(1)}, u32[]{:S(2)}, u32[]{:S(2)}) collective-permute-start(s32[192]{0:T(256)} %get-tuple-element.714), channel_id=1, source_target_pairs={{0,1},{1,2},{2,3},{3,4},{4,5},{5,6},{6,7},{7,8},{8,9},{9,10},{10,1... | collective-permute-start | bytes 2312 | tf_op jit(solution)/shard_map/while/body/eval_jaxpr/ppermute | solution.py:21
  182.2 37.6 %collective-permute-start.1 = (bf16[192,1024]{1,0:T(8,128)(2,1)}, bf16[192,1024]{1,0:T(8,128)(2,1)S(1)}, u32[]{:S(2)}, u32[]{:S(2)}) collective-permute-start(bf16[192,1024]{1,0:T(8,128)(2,1)} %get-tuple-element.712), channel_id=1, source_target_pairs={{0,1},{1,2},{2,3},{3,4},{4,5},{5,6},{6,7},{7,8},{8,9},{9,10},{10,1... | collective-permute-start | bytes 1179656 | tf_op jit(solution)/shard_map/while/body/eval_jaxpr/ppermute | solution.py:21
  186.3 33.5 %collective-permute-start.2 = (bf16[192,1024]{1,0:T(8,128)(2,1)}, bf16[192,1024]{1,0:T(8,128)(2,1)}, u32[]{:S(2)}, u32[]{:S(2)}) collective-permute-start(bf16[192,1024]{1,0:T(8,128)(2,1)} %copy-done.15), channel_id=1, source_target_pairs={{0,1},{1,2},{2,3},{3,4},{4,5},{5,6},{6,7},{7,8},{8,9},{9,10},{10,1... | collective-permute-start | bytes 1179656 | tf_op jit(solution)/shard_map/while/body/eval_jaxpr/ppermute | solution.py:21
  190.4 28.7 %collective-permute-start = (s32[192]{0:T(256)}, s32[192]{0:T(256)S(1)}, u32[]{:S(2)}, u32[]{:S(2)}) collective-permute-start(s32[192]{0:T(256)} %get-tuple-element.714), channel_id=1, source_target_pairs={{0,1},{1,2},{2,3},{3,4},{4,5},{5,6},{6,7},{7,8},{8,9},{9,10},{10,1... | collective-permute-start | bytes 2312 | tf_op jit(solution)/shard_map/while/body/eval_jaxpr/ppermute | solution.py:21
  231.4 38.5 %collective-permute-start.1 = (bf16[192,1024]{1,0:T(8,128)(2,1)}, bf16[192,1024]{1,0:T(8,128)(2,1)S(1)}, u32[]{:S(2)}, u32[]{:S(2)}) collective-permute-start(bf16[192,1024]{1,0:T(8,128)(2,1)} %get-tuple-element.712), channel_id=1, source_target_pairs={{0,1},{1,2},{2,3},{3,4},{4,5},{5,6},{6,7},{7,8},{8,9},{9,10},{10,1... | collective-permute-start | bytes 1179656 | tf_op jit(solution)/shard_map/while/body/eval_jaxpr/ppermute | solution.py:21
  235.5 34.4 %collective-permute-start.2 = (bf16[192,1024]{1,0:T(8,128)(2,1)}, bf16[192,1024]{1,0:T(8,128)(2,1)}, u32[]{:S(2)}, u32[]{:S(2)}) collective-permute-start(bf16[192,1024]{1,0:T(8,128)(2,1)} %copy-done.15), channel_id=1, source_target_pairs={{0,1},{1,2},{2,3},{3,4},{4,5},{5,6},{6,7},{7,8},{8,9},{9,10},{10,1... | collective-permute-start | bytes 1179656 | tf_op jit(solution)/shard_map/while/body/eval_jaxpr/ppermute | solution.py:21
  239.7 29.5 %collective-permute-start = (s32[192]{0:T(256)}, s32[192]{0:T(256)S(1)}, u32[]{:S(2)}, u32[]{:S(2)}) collective-permute-start(s32[192]{0:T(256)} %get-tuple-element.714), channel_id=1, source_target_pairs={{0,1},{1,2},{2,3},{3,4},{4,5},{5,6},{6,7},{7,8},{8,9},{9,10},{10,1... | collective-permute-start | bytes 2312 | tf_op jit(solution)/shard_map/while/body/eval_jaxpr/ppermute | solution.py:21
  281.5 38.2 %collective-permute-start.1 = (bf16[192,1024]{1,0:T(8,128)(2,1)}, bf16[192,1024]{1,0:T(8,128)(2,1)S(1)}, u32[]{:S(2)}, u32[]{:S(2)}) collective-permute-start(bf16[192,1024]{1,0:T(8,128)(2,1)} %get-tuple-element.712), channel_id=1, source_target_pairs={{0,1},{1,2},{2,3},{3,4},{4,5},{5,6},{6,7},{7,8},{8,9},{9,10},{10,1... | collective-permute-start | bytes 1179656 | tf_op jit(solution)/shard_map/while/body/eval_jaxpr/ppermute | solution.py:21
  285.6 34.2 %collective-permute-start.2 = (bf16[192,1024]{1,0:T(8,128)(2,1)}, bf16[192,1024]{1,0:T(8,128)(2,1)}, u32[]{:S(2)}, u32[]{:S(2)}) collective-permute-start(bf16[192,1024]{1,0:T(8,128)(2,1)} %copy-done.15), channel_id=1, source_target_pairs={{0,1},{1,2},{2,3},{3,4},{4,5},{5,6},{6,7},{7,8},{8,9},{9,10},{10,1... | collective-permute-start | bytes 1179656 | tf_op jit(solution)/shard_map/while/body/eval_jaxpr/ppermute | solution.py:21
  289.8 29.2 %collective-permute-start = (s32[192]{0:T(256)}, s32[192]{0:T(256)S(1)}, u32[]{:S(2)}, u32[]{:S(2)}) collective-permute-start(s32[192]{0:T(256)} %get-tuple-element.714), channel_id=1, source_target_pairs={{0,1},{1,2},{2,3},{3,4},{4,5},{5,6},{6,7},{7,8},{8,9},{9,10},{10,1... | collective-permute-start | bytes 2312 | tf_op jit(solution)/shard_map/while/body/eval_jaxpr/ppermute | solution.py:21
  331.2 18.5 %collective-permute-start.1 = (bf16[192,1024]{1,0:T(8,128)(2,1)}, bf16[192,1024]{1,0:T(8,128)(2,1)S(1)}, u32[]{:S(2)}, u32[]{:S(2)}) collective-permute-start(bf16[192,1024]{1,0:T(8,128)(2,1)} %get-tuple-element.712), channel_id=1, source_target_pairs={{0,1},{1,2},{2,3},{3,4},{4,5},{5,6},{6,7},{7,8},{8,9},{9,10},{10,1... | collective-permute-start | bytes 1179656 | tf_op jit(solution)/shard_map/while/body/eval_jaxpr/ppermute | solution.py:21
  335.4 14.4 %collective-permute-start.2 = (bf16[192,1024]{1,0:T(8,128)(2,1)}, bf16[192,1024]{1,0:T(8,128)(2,1)}, u32[]{:S(2)}, u32[]{:S(2)}) collective-permute-start(bf16[192,1024]{1,0:T(8,128)(2,1)} %copy-done.15), channel_id=1, source_target_pairs={{0,1},{1,2},{2,3},{3,4},{4,5},{5,6},{6,7},{7,8},{8,9},{9,10},{10,1... | collective-permute-start | bytes 1179656 | tf_op jit(solution)/shard_map/while/body/eval_jaxpr/ppermute | solution.py:21
  339.6 9.4 collective-permute-start
  361.2 21.3 %collective-permute-start.1 = (bf16[192,1024]{1,0:T(8,128)(2,1)}, bf16[192,1024]{1,0:T(8,128)(2,1)S(1)}, u32[]{:S(2)}, u32[]{:S(2)}) collective-permute-start(bf16[192,1024]{1,0:T(8,128)(2,1)} %get-tuple-element.712), channel_id=1, source_target_pairs={{0,1},{1,2},{2,3},{3,4},{4,5},{5,6},{6,7},{7,8},{8,9},{9,10},{10,1... | collective-permute-start | bytes 1179656 | tf_op jit(solution)/shard_map/while/body/eval_jaxpr/ppermute | solution.py:21
  366.4 16.3 %collective-permute-start.2 = (bf16[192,1024]{1,0:T(8,128)(2,1)}, bf16[192,1024]{1,0:T(8,128)(2,1)}, u32[]{:S(2)}, u32[]{:S(2)}) collective-permute-start(bf16[192,1024]{1,0:T(8,128)(2,1)} %copy-done.15), channel_id=1, source_target_pairs={{0,1},{1,2},{2,3},{3,4},{4,5},{5,6},{6,7},{7,8},{8,9},{9,10},{10,1... | collective-permute-start | bytes 1179656 | tf_op jit(solution)/shard_map/while/body/eval_jaxpr/ppermute | solution.py:21
  373.3 8.5 collective-permute-start
  394.1 20.8 %collective-permute-start.1 = (bf16[192,1024]{1,0:T(8,128)(2,1)}, bf16[192,1024]{1,0:T(8,128)(2,1)S(1)}, u32[]{:S(2)}, u32[]{:S(2)}) collective-permute-start(bf16[192,1024]{1,0:T(8,128)(2,1)} %get-tuple-element.712), channel_id=1, source_target_pairs={{0,1},{1,2},{2,3},{3,4},{4,5},{5,6},{6,7},{7,8},{8,9},{9,10},{10,1... | collective-permute-start | bytes 1179656 | tf_op jit(solution)/shard_map/while/body/eval_jaxpr/ppermute | solution.py:21
  399.4 15.5 %collective-permute-start.2 = (bf16[192,1024]{1,0:T(8,128)(2,1)}, bf16[192,1024]{1,0:T(8,128)(2,1)}, u32[]{:S(2)}, u32[]{:S(2)}) collective-permute-start(bf16[192,1024]{1,0:T(8,128)(2,1)} %copy-done.15), channel_id=1, source_target_pairs={{0,1},{1,2},{2,3},{3,4},{4,5},{5,6},{6,7},{7,8},{8,9},{9,10},{10,1... | collective-permute-start | bytes 1179656 | tf_op jit(solution)/shard_map/while/body/eval_jaxpr/ppermute | solution.py:21
  405.6 8.5 collective-permute-start
  426.3 19.4 %collective-permute-start.1 = (bf16[192,1024]{1,0:T(8,128)(2,1)}, bf16[192,1024]{1,0:T(8,128)(2,1)S(1)}, u32[]{:S(2)}, u32[]{:S(2)}) collective-permute-start(bf16[192,1024]{1,0:T(8,128)(2,1)} %get-tuple-element.712), channel_id=1, source_target_pairs={{0,1},{1,2},{2,3},{3,4},{4,5},{5,6},{6,7},{7,8},{8,9},{9,10},{10,1... | collective-permute-start | bytes 1179656 | tf_op jit(solution)/shard_map/while/body/eval_jaxpr/ppermute | solution.py:21
  431.2 14.6 %collective-permute-start.2 = (bf16[192,1024]{1,0:T(8,128)(2,1)}, bf16[192,1024]{1,0:T(8,128)(2,1)}, u32[]{:S(2)}, u32[]{:S(2)}) collective-permute-start(bf16[192,1024]{1,0:T(8,128)(2,1)} %copy-done.15), channel_id=1, source_target_pairs={{0,1},{1,2},{2,3},{3,4},{4,5},{5,6},{6,7},{7,8},{8,9},{9,10},{10,1... | collective-permute-start | bytes 1179656 | tf_op jit(solution)/shard_map/while/body/eval_jaxpr/ppermute | solution.py:21
  436.7 8.4 collective-permute-start
  457.3 17.7 %collective-permute-start.1 = (bf16[192,1024]{1,0:T(8,128)(2,1)}, bf16[192,1024]{1,0:T(8,128)(2,1)S(1)}, u32[]{:S(2)}, u32[]{:S(2)}) collective-permute-start(bf16[192,1024]{1,0:T(8,128)(2,1)} %get-tuple-element.712), channel_id=1, source_target_pairs={{0,1},{1,2},{2,3},{3,4},{4,5},{5,6},{6,7},{7,8},{8,9},{9,10},{10,1... | collective-permute-start | bytes 1179656 | tf_op jit(solution)/shard_map/while/body/eval_jaxpr/ppermute | solution.py:21
  461.4 13.6 %collective-permute-start.2 = (bf16[192,1024]{1,0:T(8,128)(2,1)}, bf16[192,1024]{1,0:T(8,128)(2,1)}, u32[]{:S(2)}, u32[]{:S(2)}) collective-permute-start(bf16[192,1024]{1,0:T(8,128)(2,1)} %copy-done.15), channel_id=1, source_target_pairs={{0,1},{1,2},{2,3},{3,4},{4,5},{5,6},{6,7},{7,8},{8,9},{9,10},{10,1... | collective-permute-start | bytes 1179656 | tf_op jit(solution)/shard_map/while/body/eval_jaxpr/ppermute | solution.py:21
  466.6 7.7 collective-permute-start
  486.5 16.2 %collective-permute-start.1 = (bf16[192,1024]{1,0:T(8,128)(2,1)}, bf16[192,1024]{1,0:T(8,128)(2,1)S(1)}, u32[]{:S(2)}, u32[]{:S(2)}) collective-permute-start(bf16[192,1024]{1,0:T(8,128)(2,1)} %get-tuple-element.712), channel_id=1, source_target_pairs={{0,1},{1,2},{2,3},{3,4},{4,5},{5,6},{6,7},{7,8},{8,9},{9,10},{10,1... | collective-permute-start | bytes 1179656 | tf_op jit(solution)/shard_map/while/body/eval_jaxpr/ppermute | solution.py:21
  490.6 12.3 %collective-permute-start.2 = (bf16[192,1024]{1,0:T(8,128)(2,1)}, bf16[192,1024]{1,0:T(8,128)(2,1)}, u32[]{:S(2)}, u32[]{:S(2)}) collective-permute-start(bf16[192,1024]{1,0:T(8,128)(2,1)} %copy-done.15), channel_id=1, source_target_pairs={{0,1},{1,2},{2,3},{3,4},{4,5},{5,6},{6,7},{7,8},{8,9},{9,10},{10,1... | collective-permute-start | bytes 1179656 | tf_op jit(solution)/shard_map/while/body/eval_jaxpr/ppermute | solution.py:21
  494.9 7.2 collective-permute-start
  514.3 15.1 %collective-permute-start.1 = (bf16[192,1024]{1,0:T(8,128)(2,1)}, bf16[192,1024]{1,0:T(8,128)(2,1)S(1)}, u32[]{:S(2)}, u32[]{:S(2)}) collective-permute-start(bf16[192,1024]{1,0:T(8,128)(2,1)} %get-tuple-element.712), channel_id=1, source_target_pairs={{0,1},{1,2},{2,3},{3,4},{4,5},{5,6},{6,7},{7,8},{8,9},{9,10},{10,1... | collective-permute-start | bytes 1179656 | tf_op jit(solution)/shard_map/while/body/eval_jaxpr/ppermute | solution.py:21
  518.3 11.1 %collective-permute-start.2 = (bf16[192,1024]{1,0:T(8,128)(2,1)}, bf16[192,1024]{1,0:T(8,128)(2,1)}, u32[]{:S(2)}, u32[]{:S(2)}) collective-permute-start(bf16[192,1024]{1,0:T(8,128)(2,1)} %copy-done.15), channel_id=1, source_target_pairs={{0,1},{1,2},{2,3},{3,4},{4,5},{5,6},{6,7},{7,8},{8,9},{9,10},{10,1... | collective-permute-start | bytes 1179656 | tf_op jit(solution)/shard_map/while/body/eval_jaxpr/ppermute | solution.py:21
  522.2 6.5 collective-permute-start
  540.9 13.9 %collective-permute-start.1 = (bf16[192,1024]{1,0:T(8,128)(2,1)}, bf16[192,1024]{1,0:T(8,128)(2,1)S(1)}, u32[]{:S(2)}, u32[]{:S(2)}) collective-permute-start(bf16[192,1024]{1,0:T(8,128)(2,1)} %get-tuple-element.712), channel_id=1, source_target_pairs={{0,1},{1,2},{2,3},{3,4},{4,5},{5,6},{6,7},{7,8},{8,9},{9,10},{10,1... | collective-permute-start | bytes 1179656 | tf_op jit(solution)/shard_map/while/body/eval_jaxpr/ppermute | solution.py:21
  544.9 9.9 collective-permute-start.2
  548.1 6.0 collective-permute-start
  566.3 13.7 %collective-permute-start.1 = (bf16[192,1024]{1,0:T(8,128)(2,1)}, bf16[192,1024]{1,0:T(8,128)(2,1)S(1)}, u32[]{:S(2)}, u32[]{:S(2)}) collective-permute-start(bf16[192,1024]{1,0:T(8,128)(2,1)} %get-tuple-element.712), channel_id=1, source_target_pairs={{0,1},{1,2},{2,3},{3,4},{4,5},{5,6},{6,7},{7,8},{8,9},{9,10},{10,1... | collective-permute-start | bytes 1179656 | tf_op jit(solution)/shard_map/while/body/eval_jaxpr/ppermute | solution.py:21
  570.1 9.9 collective-permute-start.2
  574.8 4.5 collective-permute-start
  591.5 15.5 %collective-permute-start.1 = (bf16[192,1024]{1,0:T(8,128)(2,1)}, bf16[192,1024]{1,0:T(8,128)(2,1)S(1)}, u32[]{:S(2)}, u32[]{:S(2)}) collective-permute-start(bf16[192,1024]{1,0:T(8,128)(2,1)} %get-tuple-element.712), channel_id=1, source_target_pairs={{0,1},{1,2},{2,3},{3,4},{4,5},{5,6},{6,7},{7,8},{8,9},{9,10},{10,1... | collective-permute-start | bytes 1179656 | tf_op jit(solution)/shard_map/while/body/eval_jaxpr/ppermute | solution.py:21
  597.2 10.0 collective-permute-start.2
  602.1 4.3 collective-permute-start
  671.0 259.6 %copy-start.17 = (f32[64,256]{1,0:T(8,128)S(1)}, f32[64,256]{1,0:T(8,128)}, u32[]{:S(2)}) copy-start(f32[64,256]{1,0:T(8,128)} %copy-done.16) | copy-start | bytes 196612
  (86 other events, 667.1 us)
Sparse Core Ops, SparseCore 0:
  28.1 139.8 all-gather.5
  170.1 164.4 all-gather.7
where the time goes:
time: 1080 us; the launch traced here: 1060 us
  local copies, waits for them, and re-layouts  221 us (20%)
  starting transfers between devices  175 us (16%)
  waiting for transfers between devices  164 us (15%)
  matrix products  159 us (15%)
  other arithmetic  150 us (14%)
  blocking collectives  145 us (13%)
  loops' own time  34.4 us (3%)
  between operations  15.5 us (1%)
    ppermute x45, starting transfers between devices, from_behind(): return lax.ppermute(block, axis, route)  175 us
    ppermute x45, waiting for transfers between devices, from_behind(): return lax.ppermute(block, axis, route)  164 us
    dynamic_slice x64, local copies, waits for them, and re-layouts, step(): part[k].astype(own.dtype)  115 us
    select_n x16, other arithmetic, step(): return jax.tree.map(lambda a, b: jnp.where(reached, a, b), new, before)  112 us
    psum x1, blocking collectives, on_device(): grand = lax.psum(grad_near + grad_far, ('dp', 'ctx'))  81.4 us
    while x210, local copies, waits for them, and re-layouts  71.8 us
    dot_general x16, matrix products, attend_tile(): jnp.einsum('kvuc,ckw->ukvw', exponent_weight.astype(jnp.bfloat16), value_...  46.1 us
    dot_general x16, matrix products, attend_tile(): jnp.einsum('fkhu,nku->khfn', query_head_count, key_head_count, preferred_...  43.9 us
  transfers between devices with their start and end apart: 47, of which 15 were waited for; matrix products, arithmetic and copies ran while one was open for 21% of the time, Pallas kernels for 0%

commit v1 on v0

v1 whole, which is shorter than its diff:
```python
import functools
import math

import jax
import jax.numpy as jnp
from jax import lax
from jax.experimental import pallas as pl
from jax.experimental.pallas import tpu as pltpu
from jax.sharding import PartitionSpec as P

Q_HEADS = 32
KV_HEADS = 8
REP = Q_HEADS // KV_HEADS
WIDTH = 128
SSD_HEADS = 64
HEAD_P = 64
STATE = 128
GROUPS = 8
PER = SSD_HEADS // GROUPS
GW = PER * HEAD_P
COLS = 4
ROWS = 4
KVW = 2 * KV_HEADS * WIDTH + WIDTH
FAR_BELOW = -1e30
MESH = pl.DeviceIdType.MESH

OWN, P1, P2, AB1, AB3, AB2, BC1, BC3, BC2 = range(9)
BACK = (0, 4, 8, 1, 3, 2, 5, 7, 6)

f32, bf16 = jnp.float32, jnp.bfloat16


def dot(a, b, ca, cb, precision=None):
    return lax.dot_general(
        a, b, (((ca,), (cb,)), ((), ())), precision=precision, preferred_element_type=f32
    )


def kernel(
    q_ref, k_ref, v_ref, seg_ref, x_ref, b_ref, c_ref, logs_ref, skip_ref, g_ref,
    ao_ref, mo_ref, dgn_ref, dgf_ref,
    kvb, qs, acc, mrow, lrow, bias, st_own, st_row, meta_own, meta_row,
    r_out, r_meta, r_in, r_meta_in, f_out, f_in, d_ref, dh_ref, fexp_ref, near_ref,
    kv_ss, kv_rs, a_ss, a_rs, am_ss, am_rs, r_ss, r_rs, rm_ss, rm_rs, f_ss, f_rs,
):
    count = q_ref.shape[0]
    me = lax.axis_index("ctx")
    z, x = me // COLS, me % COLS

    def dev(dz, dx):
        return {"ctx": ((z + dz) % ROWS) * COLS + (x + dx) % COLS}

    barrier = pltpu.get_barrier_semaphore()
    partners = [(0, 1), (0, 2), (0, 3), (1, 0), (2, 0), (3, 0)]
    for dz, dx in partners:
        pl.semaphore_signal(barrier, inc=1, device_id=dev(dz, dx), device_id_type=MESH)

    segrow = seg_ref[...].astype(f32)
    rr = lax.broadcasted_iota(jnp.int32, (count, count), 0)
    cc = lax.broadcasted_iota(jnp.int32, (count, count), 1)
    eye = rr == cc
    segcol = jnp.sum(jnp.where(eye, segrow, 0.0), axis=1, keepdims=True)
    lane = lax.broadcasted_iota(jnp.int32, (count, WIDTH), 1).astype(f32)
    onehot = jnp.where(lane == segcol, 1.0, 0.0).astype(bf16)
    other = jnp.where((lane != segcol) & (lane < 8.0), FAR_BELOW, 0.0).astype(bf16)
    kvb[OWN, :, : KV_HEADS * WIDTH] = k_ref[...]
    kvb[OWN, :, KV_HEADS * WIDTH : 2 * KV_HEADS * WIDTH] = v_ref[...]
    kvb[OWN, :, 2 * KV_HEADS * WIDTH :] = other

    pl.semaphore_wait(barrier, len(partners))

    def kv_copy(src, slot, dz, dx):
        return pltpu.make_async_remote_copy(
            src_ref=kvb.at[src], dst_ref=kvb.at[slot], send_sem=kv_ss.at[slot],
            recv_sem=kv_rs.at[slot], device_id=dev(dz, dx), device_id_type=MESH,
        )

    @pl.when(z < 3)
    def _():
        kv_copy(OWN, P1, 1, 0).start()

    for slot, d in ((AB1, 1), (AB3, 3), (AB2, 2)):
        @pl.when(x + d < COLS)
        def _(slot=slot, d=d):
            kv_copy(OWN, slot, 0, d).start()

    @pl.when(z < 2)
    def _():
        kv_copy(OWN, P2, 2, 0).start()

    mask = (cc <= rr) & (segrow == segcol)
    upper = jnp.where(rr <= cc, 1.0, 0.0)
    eyef = jnp.where(eye, 1.0, 0.0)
    keep = jnp.where(segrow == segrow[:, count - 1 : count], 1.0, 0.0)
    live = jnp.where(segrow == segrow[:, 0:1], 1.0, 0.0)
    h16 = lax.broadcasted_iota(jnp.int32, (2 * PER, GW), 0) % PER
    spread = jnp.where(h16 == lax.broadcasted_iota(jnp.int32, (2 * PER, GW), 1) // HEAD_P, 1.0, 0.0)
    spread_bf = spread.astype(bf16)
    hi = lax.Precision.HIGHEST
    low_half = lax.broadcasted_iota(jnp.int32, (count, 2 * HEAD_P), 1) < HEAD_P
    meta_rows = lax.broadcasted_iota(jnp.int32, (8, GW), 0)
    last_own, first_own = segrow[:, count - 1 : count], segrow[:, 0:1]

    def expand(value):
        top = value.astype(bf16)
        rest = (value - top.astype(f32)).astype(bf16)
        return dot(jnp.concatenate([top, rest], axis=0), spread_bf, 0, 0)

    def mixer_group(g, _):
        cols = pl.ds(pl.multiple_of(g * GW, GW), GW)
        ncols = pl.ds(pl.multiple_of(g * STATE, STATE), STATE)
        cs = dot(logs_ref[pl.ds(pl.multiple_of(g * PER, PER), PER), :], upper, 1, 0, hi)
        cst = dot(eyef, cs, 1, 1, hi)
        span = cs[:, count - 1 : count]
        tail = span - cs
        e = jnp.exp(tail) * keep
        f = jnp.exp(cs) * live
        xg, gg = x_ref[:, cols], g_ref[:, cols]
        bg, cg = b_ref[:, ncols].astype(bf16), c_ref[:, ncols].astype(bf16)
        right = jnp.concatenate([(xg * expand(e)).astype(bf16), (xg * expand(e * tail)).astype(bf16)], axis=1)
        sh = dot(bg, right, 0, 0).astype(bf16)
        st_own[g // 2, g % 2] = sh[:, :GW]
        st_own[g // 2, 2 + g % 2] = sh[:, GW:]
        fe = expand(f)
        fexp_ref[g] = fe
        right = jnp.concatenate([(gg * fe).astype(bf16), (gg * expand(f * cs)).astype(bf16)], axis=1)
        dd = dot(cg, right, 0, 0)
        d_ref[g] = dd[:, :GW]
        dh_ref[g] = dd[:, GW:]
        span_row = jnp.sum(spread[:PER] * span, axis=0, keepdims=True)
        meta = jnp.where(meta_rows == 0, span_row, jnp.where(meta_rows == 1, last_own, first_own))
        meta_own[g // 2, :, pl.ds(pl.multiple_of((g % 2) * GW, GW), GW)] = meta
        inner = dot(cg, bg, 1, 1)
        sums = []
        for pair in range(PER // 2):
            lanes = slice(pair * 2 * HEAD_P, (pair + 1) * 2 * HEAD_P)
            xp, gp = xg[:, lanes], gg[:, lanes]
            xpb, gpb = xp.astype(bf16), gp.astype(bf16)
            near = None
            for half in range(2):
                j = pair * 2 + half
                mine = low_half if half == 0 else jnp.logical_not(low_half)
                gap = jnp.where(mask, cst[:, j : j + 1] - cs[j : j + 1, :], FAR_BELOW)
                weight = jnp.exp(gap) * inner
                pairs = dot(jnp.where(mine, gpb, jnp.zeros_like(gpb)), xpb, 1, 1)
                sums.append(jnp.sum(weight * gap * pairs, axis=0, keepdims=True))
                part = dot(weight.astype(bf16), jnp.where(mine, xpb, jnp.zeros_like(xpb)), 1, 0)
                near = part if near is None else near + part
            at = pl.ds(pl.multiple_of(g * GW + pair * 2 * HEAD_P, 2 * HEAD_P), 2 * HEAD_P)
            near_ref[:, at] = near + xp * skip_ref[:, at]
        dgn_ref[pl.ds(pl.multiple_of(g * PER, PER), PER), :] = jnp.concatenate(sums, axis=0)
        return 0

    lax.fori_loop(0, GROUPS, mixer_group, 0)

    def a_copy(d):
        to = (x + d) % COLS
        return pltpu.make_async_remote_copy(
            src_ref=st_own.at[to], dst_ref=st_row.at[x], send_sem=a_ss.at[d - 1],
            recv_sem=a_rs.at[d - 1], device_id=dev(0, d), device_id_type=MESH,
        )

    def am_copy(d):
        to = (x + d) % COLS
        return pltpu.make_async_remote_copy(
            src_ref=meta_own.at[to], dst_ref=meta_row.at[x], send_sem=am_ss.at[d - 1],
            recv_sem=am_rs.at[d - 1], device_id=dev(0, d), device_id_type=MESH,
        )

    for d in (1, 3, 2):
        am_copy(d).start()
        a_copy(d).start()
    st_row[x] = st_own[x]
    meta_row[x] = meta_own[x]

    for h in range(KV_HEADS):
        for r in range(REP):
            head = h * REP + r
            qs[h, r * count : (r + 1) * count, :WIDTH] = q_ref[:, head * WIDTH : (head + 1) * WIDTH]
            qs[h, r * count : (r + 1) * count, WIDTH:] = onehot
    causal = jnp.where(rr <= cc, 0.0, FAR_BELOW)
    bias[...] = jnp.concatenate([causal] * REP, axis=1)
    scale = math.log2(math.e) / math.sqrt(WIDTH)

    def scores(slot, h):
        at = pl.ds(pl.multiple_of(h * WIDTH, WIDTH), WIDTH)
        kk = jnp.concatenate([kvb[slot, :, at], kvb[slot, :, 2 * KV_HEADS * WIDTH :]], axis=1)
        return dot(kk, qs[h], 1, 1)

    def values_of(slot, h):
        return kvb[slot, :, pl.ds(pl.multiple_of((KV_HEADS + h) * WIDTH, WIDTH), WIDTH)]

    def own_head(h, _):
        s = scores(OWN, h) + bias[...]
        top = jnp.max(s, axis=0, keepdims=True)
        w = jnp.exp2((s - top) * scale)
        mrow[pl.ds(h, 1), :] = top
        lrow[pl.ds(h, 1), :] = jnp.sum(w, axis=0, keepdims=True)
        acc[h] = dot(values_of(OWN, h), w.astype(bf16), 0, 0)
        return 0

    lax.fori_loop(0, KV_HEADS, own_head, 0)

    def attend(slot):
        def head(h, _):
            s = scores(slot, h)
            before = mrow[pl.ds(h, 1), :]
            top = jnp.maximum(before, jnp.max(s, axis=0, keepdims=True))
            w = jnp.exp2((s - top) * scale)
            fade = jnp.exp2((before - top) * scale)
            mrow[pl.ds(h, 1), :] = top
            lrow[pl.ds(h, 1), :] = lrow[pl.ds(h, 1), :] * fade + jnp.sum(w, axis=0, keepdims=True)
            acc[h] = acc[h] * fade + dot(values_of(slot, h), w.astype(bf16), 0, 0)
            return 0

        lax.fori_loop(0, KV_HEADS, head, 0)

    def arrive(slot):
        kv_copy(OWN, slot, 0, 1).wait_recv()

    @pl.when(z >= 1)
    def _():
        arrive(P1)
        for slot, d in ((AB1, 1), (AB3, 3), (AB2, 2)):
            @pl.when(x + d >= COLS)
            def _(slot=slot, d=d):
                kv_copy(P1, slot, 0, d).start()
        for slot, d in ((BC1, 1), (BC3, 3)):
            @pl.when(x + d < COLS)
            def _(slot=slot, d=d):
                kv_copy(P1, slot, 0, d).start()

    for d in (1, 3, 2):
        am_copy(d).wait_recv()
        a_copy(d).wait_recv()

    def row_meta(k, c, at):
        return meta_row[k, at : at + 1, c * GW : (c + 1) * GW]

    for c in range(2):
        s, hat = st_row[0, c].astype(f32), st_row[0, 2 + c].astype(f32)
        total, last = row_meta(0, c, 0), row_meta(0, c, 1)
        for k in range(1, COLS):
            span, after = row_meta(k, c, 0), row_meta(k, c, 1)
            fade = jnp.where(last == after, jnp.exp(span), 0.0)
            hat = fade * (hat + span * s) + st_row[k, 2 + c].astype(f32)
            s = fade * s + st_row[k, c].astype(f32)
            total, last = total + span, after
        r_out[c] = s.astype(bf16)
        r_out[2 + c] = hat.astype(bf16)
        r_meta[:, c * GW : (c + 1) * GW] = jnp.where(meta_rows == 0, total, last)

    def r_copy(dz):
        return pltpu.make_async_remote_copy(
            src_ref=r_out, dst_ref=r_in.at[dz - 1], send_sem=r_ss.at[dz - 1],
            recv_sem=r_rs.at[dz - 1], device_id=dev(dz, 0), device_id_type=MESH,
        )

    def rm_copy(dz):
        return pltpu.make_async_remote_copy(
            src_ref=r_meta, dst_ref=r_meta_in.at[dz - 1], send_sem=rm_ss.at[dz - 1],
            recv_sem=rm_rs.at[dz - 1], device_id=dev(dz, 0), device_id_type=MESH,
        )

    for dz in (1, 2):
        @pl.when(z + dz < ROWS)
        def _(dz=dz):
            rm_copy(dz).start()
            r_copy(dz).start()

        @pl.when(z - dz < 0)
        def _(dz=dz):
            r_in[dz - 1] = jnp.zeros_like(r_in[dz - 1])
            r_meta_in[dz - 1] = jnp.full_like(r_meta_in[dz - 1], -1.0)

    for slot in (AB1, AB3):
        @pl.when(me >= BACK[slot])
        def _(slot=slot):
            arrive(slot)
            attend(slot)

    @pl.when(z >= 2)
    def _():
        arrive(P2)
        for slot, d in ((BC1, 1), (BC3, 3)):
            @pl.when(x + d >= COLS)
            def _(slot=slot, d=d):
                kv_copy(P2, slot, 0, d).start()

    @pl.when(me >= BACK[AB2])
    def _():
        arrive(AB2)

        @pl.when(z < 3)
        def _():
            kv_copy(AB2, BC2, 1, 0).start()

        attend(AB2)

    for dz in (1, 2):
        @pl.when(z - dz >= 0)
        def _(dz=dz):
            rm_copy(dz).wait_recv()
            r_copy(dz).wait_recv()

    for c in range(2):
        lanes = slice(c * GW, (c + 1) * GW)
        span, last = r_meta_in[0, 0:1, lanes], r_meta_in[0, 1:2, lanes]
        fade = jnp.where(r_meta_in[1, 1:2, lanes] == last, jnp.exp(span), 0.0)
        s2, hat2 = r_in[1, c].astype(f32), r_in[1, 2 + c].astype(f32)
        hat = fade * (hat2 + span * s2) + r_in[0, 2 + c].astype(f32)
        s = fade * s2 + r_in[0, c].astype(f32)
        for k in range(COLS):
            goes_on = jnp.where(row_meta(k, c, 2) == last, 1.0, 0.0)
            f_out[k, c] = (s * goes_on).astype(bf16)
            f_out[k, 2 + c] = (hat * goes_on).astype(bf16)
            if k < COLS - 1:
                span, after = row_meta(k, c, 0), row_meta(k, c, 1)
                fade = jnp.where(last == after, jnp.exp(span), 0.0)
                hat = fade * (hat + span * s) + st_row[k, 2 + c].astype(f32)
                s = fade * s + st_row[k, c].astype(f32)
                last = after

    def f_copy(d):
        to = (x + d) % COLS
        return pltpu.make_async_remote_copy(
            src_ref=f_out.at[to], dst_ref=f_in.at[x], send_sem=f_ss.at[d - 1],
            recv_sem=f_rs.at[d - 1], device_id=dev(0, d), device_id_type=MESH,
        )

    for d in (1, 3, 2):
        f_copy(d).start()
    f_in[x] = f_out[x]

    @pl.when(me >= BACK[P1])
    def _():
        attend(P1)

    @pl.when(me >= BACK[P2])
    def _():
        attend(P2)

    for slot in (BC1, BC3, BC2):
        @pl.when(me >= BACK[slot])
        def _(slot=slot):
            arrive(slot)
            attend(slot)

    for d in (1, 3, 2):
        f_copy(d).wait_recv()

    def far_group(g, _):
        cols = pl.ds(pl.multiple_of(g * GW, GW), GW)
        ncols = pl.ds(pl.multiple_of(g * STATE, STATE), STATE)
        s_in, hat_in = f_in[g // 2, g % 2], f_in[g // 2, 2 + g % 2]
        far = dot(c_ref[:, ncols].astype(bf16), s_in, 1, 0) * fexp_ref[g]
        mo_ref[:, cols] = (near_ref[:, cols] + far).astype(bf16)
        terms = hat_in.astype(f32) * d_ref[g] + s_in.astype(f32) * dh_ref[g]
        dgf_ref[pl.ds(g, 1), :] = jnp.sum(terms, axis=0, keepdims=True)
        return 0

    lax.fori_loop(0, GROUPS, far_group, 0)

    for h in range(KV_HEADS):
        out = (acc[h] / lrow[h : h + 1, :]).T.astype(bf16)
        for r in range(REP):
            head = h * REP + r
            ao_ref[:, head * WIDTH : (head + 1) * WIDTH] = out[r * count : (r + 1) * count]

    @pl.when(z < 3)
    def _():
        kv_copy(OWN, P1, 1, 0).wait_send()

    @pl.when(z < 2)
    def _():
        kv_copy(OWN, P2, 2, 0).wait_send()

    for slot, d in ((AB1, 1), (AB3, 3), (AB2, 2)):
        @pl.when((x + d < COLS) | (z >= 1))
        def _(slot=slot, d=d):
            kv_copy(OWN, slot, 0, d).wait_send()

    for slot, d in ((BC1, 1), (BC3, 3)):
        @pl.when(z >= 1 + (x + d) // COLS)
        def _(slot=slot, d=d):
            kv_copy(OWN, slot, 0, d).wait_send()

    @pl.when((me >= BACK[AB2]) & (z < 3))
    def _():
        kv_copy(OWN, BC2, 1, 0).wait_send()

    for d in (1, 3, 2):
        am_copy(d).wait_send()
        a_copy(d).wait_send()
        f_copy(d).wait_send()
    for dz in (1, 2):
        @pl.when(z + dz < ROWS)
        def _(dz=dz):
            rm_copy(dz).wait_send()
            r_copy(dz).wait_send()


def fused(q, k, v, seg, x, b, c, logs, skip, g):
    count = q.shape[0]
    vmem = pl.BlockSpec(memory_space=pltpu.VMEM)
    dma = pltpu.SemaphoreType.DMA
    return pl.pallas_call(
        kernel,
        out_shape=(
            jax.ShapeDtypeStruct((count, Q_HEADS * WIDTH), bf16),
            jax.ShapeDtypeStruct((count, SSD_HEADS * HEAD_P), bf16),
            jax.ShapeDtypeStruct((SSD_HEADS, count), f32),
            jax.ShapeDtypeStruct((GROUPS, GW), f32),
        ),
        in_specs=[vmem] * 10,
        out_specs=(vmem,) * 4,
        scratch_shapes=[
            pltpu.VMEM((9, count, KVW), bf16),
            pltpu.VMEM((KV_HEADS, REP * count, 2 * WIDTH), bf16),
            pltpu.VMEM((KV_HEADS, WIDTH, REP * count), f32),
            pltpu.VMEM((KV_HEADS, REP * count), f32),
            pltpu.VMEM((KV_HEADS, REP * count), f32),
            pltpu.VMEM((count, REP * count), f32),
            pltpu.VMEM((COLS, 4, STATE, GW), bf16),
            pltpu.VMEM((COLS, 4, STATE, GW), bf16),
            pltpu.VMEM((COLS, 8, 2 * GW), f32),
            pltpu.VMEM((COLS, 8, 2 * GW), f32),
            pltpu.VMEM((4, STATE, GW), bf16),
            pltpu.VMEM((8, 2 * GW), f32),
            pltpu.VMEM((2, 4, STATE, GW), bf16),
            pltpu.VMEM((2, 8, 2 * GW), f32),
            pltpu.VMEM((COLS, 4, STATE, GW), bf16),
            pltpu.VMEM((COLS, 4, STATE, GW), bf16),
            pltpu.VMEM((GROUPS, STATE, GW), f32),
            pltpu.VMEM((GROUPS, STATE, GW), f32),
            pltpu.VMEM((GROUPS, count, GW), f32),
            pltpu.VMEM((count, SSD_HEADS * HEAD_P), f32),
            dma((9,)), dma((9,)),
            dma((3,)), dma((3,)), dma((3,)), dma((3,)),
            dma((2,)), dma((2,)), dma((2,)), dma((2,)),
            dma((3,)), dma((3,)),
        ],
        compiler_params=pltpu.CompilerParams(
            collective_id=0, has_side_effects=True, vmem_limit_bytes=60 * 2**20
        ),
        name="fused_mixer_attention",
    )(q, k, v, seg, x, b, c, logs, skip, g)


def on_device(
    queries, keys, values, segment_ids, ssd_input, b_matrix, c_matrix, step_size,
    decay_log, skip_gain, cotangent,
):
    count = queries.shape[1]
    logs = step_size[0] * (-jnp.exp(decay_log))[:, None]
    skip = jnp.repeat(skip_gain, HEAD_P)[None, :]
    attention, mixed, near, far = fused(
        queries[0], keys[0], values[0], segment_ids, ssd_input[0], b_matrix[0], c_matrix[0],
        logs, skip, cotangent[0],
    )
    part = jnp.sum(near, axis=1) + jnp.sum(far.reshape(SSD_HEADS, HEAD_P), axis=1)
    grand = lax.psum(part, ("dp", "ctx"))
    decay_grad = grand / (lax.axis_size("dp") * lax.axis_size("ctx") * count)
    return attention[None], mixed[None], decay_grad


def solution(mesh):
    tok = P("dp", "ctx", None)
    return jax.shard_map(
        on_device,
        mesh=mesh,
        in_specs=(tok, tok, tok, P("dp", "ctx"), tok, tok, tok, P("dp", None, "ctx"), P(), P(), tok),
        out_specs=(tok, tok, P()),
        check_vma=False,
    )
```

time: 1080 us -> 208 us (0.19); the launches traced: 1060 us -> 208 us
  local copies, waits for them, and re-layouts: 221 us -> 6.18 us
  starting transfers between devices: 175 us -> 0 us
  waiting for transfers between devices: 164 us -> 0 us
  matrix products: 159 us -> 0 us
  other arithmetic: 150 us -> 3.79 us
  Pallas kernels: 0 us -> 113 us
  blocking collectives: 145 us -> 84.7 us
  loops' own time: 34.4 us -> 0 us
  between operations: 15.5 us -> 0.65 us
    ppermute x45 -> x0, starting transfers between devices: 175 us -> none  [from_behind(): return lax.ppermute(block, axis, route)]
    ppermute x45 -> x0, waiting for transfers between devices: 164 us -> none  [from_behind(): return lax.ppermute(block, axis, route)]
    dot_general x39 -> x0, matrix products: 159 us -> none  [the longest x16 46.1 us: attend_tile(): jnp.einsum('kvuc,ckw->ukvw', exponent_weight.astype(jnp.bfloat16), value_...]
    dynamic_slice x64 -> x0, local copies, waits for them, and re-layouts: 115 us -> none  [step(): part[k].astype(own.dtype)]
    pallas_call x0 -> x1, Pallas kernels: none -> 113 us  [fused(): pl.pallas_call(kernel, out_shape=(jax.ShapeDtypeStruct((count, Q_HEADS *...]
    select_n x32 -> x0, other arithmetic: 113 us -> none  [the longest x16 112 us: step(): return jax.tree.map(lambda a, b: jnp.where(reached, a, b), new, before)]
    while x210 -> x0, local copies, waits for them, and re-layouts: 71.8 us -> none
    unnamed x1 -> x0, blocking collectives: 36.7 us -> none
  transfers between devices with their start and end apart: 47 -> 0, of which waited for: 15 -> 0; matrix products, arithmetic and copies ran while one was open for 21% -> 0% of each run, Pallas kernels for 0% -> 0%
where the time goes in v1:
time: 208 us
  Pallas kernels  113 us (54%)
  blocking collectives  84.7 us (41%)
  local copies, waits for them, and re-layouts  6.18 us (3%)
  other arithmetic  3.79 us (2%)
    pallas_call x1, Pallas kernels, fused(): pl.pallas_call(kernel, out_shape=(jax.ShapeDtypeStruct((count, Q_HEADS *...  113 us
    psum x1, blocking collectives, on_device(): grand = lax.psum(part, ('dp', 'ctx'))  84.7 us

profile of v1, /device:TPU:1, one launch (start us, length us, event | category | flops | bytes accessed | tf_op | source)
XLA Modules:
  0.0 208.0 jit_solution(9066609321125071568)
XLA Ops:
  0.6 0.7 exponential_negate_fusion
  1.3 1.5 bitcast_multiply_fusion.logs_ref
  2.8 0.7 broadcast_in_dim.10
  3.6 0.7 broadcast_in_dim_reshape.3.skip_ref
  4.3 112.7 %fused_mixer_attention.1 = (bf16[192,4096]{1,0:T(8,128)(2,1)}, bf16[192,4096]{1,0:T(8,128)(2,1)}, f32[64,192]{1,0:T(8,128)}, f32[8,512]{1,0:T(8,128)}) custom-call(bf16[192,4096]{1,0:T(8,128)(2,1)} %bitcast.15, bf16[192,1024]{1,0:T(8,128)(2,1)} %bitcast.18, bf16[192,1024]{1,0:T(8,128)(2,1)} %bitcast.19, s32[1,192]{1,0:T(1,128)} %seg_ref.1, ...), custom_call_target="tpu_custom_call" | custom-call | tf_op jit(solution)/shard_map/fused_mixer_attention/pallas_call | solution.py:407
  117.0 0.8 reshape.10
  117.8 0.1 reduce_sum.19
  117.9 1.0 reduce_sum.18
  118.9 84.7 %psum.7 = f32[64]{0:T(128)S(1)} all-reduce(f32[64]{0:T(128)S(1)} %add.5), channel_id=1, replica_groups=mesh['dp'=8,'ctx'=16] {'dp','ctx'}, use_global_device_ids=true, to_apply=%region_2.0 | all-reduce | flops 64 | bytes 512 | tf_op jit(solution)/shard_map/psum | solution.py:462
  203.5 0.5 broadcast_multiply_fusion
  204.1 0.0 copy-start
  204.1 2.8 %copy.16 = bf16[1,192,4096]{2,1,0:T(8,128)(2,1)} copy(bf16[1,192,4096]{2,1,0:T(8,128)(2,1)} %bitcast.14) | data formatting | bytes 3145728
  206.9 0.0 copy-done
  206.9 1.1 copy.17
  (1 shorter events, 0.0 us)
Async XLA Ops:
  204.1 2.8 %copy-start = (bf16[192,4096]{1,0:T(8,128)(2,1)S(1)}, bf16[192,4096]{1,0:T(8,128)(2,1)}, u32[]{:S(2)}) copy-start(bf16[192,4096]{1,0:T(8,128)(2,1)} %get-tuple-element.8) | copy-start | bytes 4718596

commit v2 on v1

v2 whole, which is shorter than its diff:
```python
import functools
import functools
import math

import jax
import jax.numpy as jnp
from jax import lax
from jax.experimental import pallas as pl
from jax.experimental.pallas import tpu as pltpu
from jax.sharding import PartitionSpec as P

Q_HEADS = 32
KV_HEADS = 8
REP = Q_HEADS // KV_HEADS
WIDTH = 128
SSD_HEADS = 64
HEAD_P = 64
STATE = 128
GROUPS = 8
PER = SSD_HEADS // GROUPS
GW = PER * HEAD_P
COLS = 4
ROWS = 4
KVW = 2 * KV_HEADS * WIDTH + WIDTH
FAR_BELOW = -1e30
MESH = pl.DeviceIdType.MESH

OWN, P1, P2, AB1, AB3, AB2, BC1, BC3, BC2, RELAY = range(10)
BACK = (0, 4, 8, 1, 3, 2, 5, 7, 6)
STEP = {AB1: 1, AB2: 2, AB3: 3, BC1: 1, BC2: 2, BC3: 3}
BEFORE = {BC1: AB1, BC2: AB2, BC3: AB3}
PLAN = (
    ("P2", 1, 2, "R"), ("P1", 0), ("AB", AB1, 0, 1), ("AB", AB1, 1, 3), ("AB2", 0, 3, "D"), ("P1", 1),
    ("AB", AB1, 1, 2), ("MIX", 0), ("MIX", 1), ("AB", AB1, 1, 1), ("BC", BC3, 0, 3, "x"),
    ("P2", 1, 3, "D"), ("P2", 0, 2, "D"), ("BC", BC1, 0, 1, "z"), ("AB", AB1, 0, 0),
    ("BC", BC1, 1, 2, "z"), ("AB", AB1, 0, 2), ("AB2", 0, 2, "F"), ("AB", AB1, 1, 0), ("AB2", 1, 0, "D"),
    ("AB", AB3, 1, 1), ("ATT", OWN), ("AB", AB3, 1, 0), ("P2", 0, 3, "F"), ("AB", AB3, 1, 2),
    ("AB", AB1, 0, 3), ("BC", BC3, 0, 2, "x"), ("BC", BC2, 0, 3, "z"), ("RT", 0), ("AB2", 1, 3, "D"),
    ("RL", 1), ("BC", BC1, 1, 1, "z"), ("AB", AB3, 0, 1), ("BC", BC3, 0, 0, "x"), ("AB2", 1, 1, "M"),
    ("ENT", 0), ("BC", BC3, 1, 2, "z"), ("BC", BC2, 1, 3, "F"), ("BC", BC1, 0, 2, "x"), ("AB", AB3, 0, 2),
    ("BC", BC3, 1, 3, "x"), ("AB2", 1, 2, "F"), ("BC", BC1, 1, 3, "x"), ("BC", BC3, 1, 0, "z"),
    ("ATT", P2), ("BC", BC3, 1, 1, "z"), ("AB2", 0, 1, "F"), ("BC", BC3, 0, 1, "x"), ("AB", AB3, 1, 3),
    ("RT", 1), ("BC", BC1, 1, 0, "x"), ("BC", BC2, 0, 2, "z"), ("BC", BC1, 0, 0, "z"), ("ATT", P1),
    ("ATT", AB1), ("AB2", 0, 0, "M"), ("BC", BC1, 0, 3, "z"), ("BC", BC2, 0, 1, "z"),
    ("BC", BC2, 1, 0, "z"), ("FAR", 0), ("ENT", 1), ("BC", BC2, 0, 0, "z"), ("ATT", AB2),
    ("BC", BC2, 1, 1, "z"), ("AB", AB3, 0, 0), ("BC", BC2, 1, 2, "z"), ("AB", AB3, 0, 3), ("ATT", BC3),
    ("ATT", BC1), ("FAR", 1), ("G1",), ("ATT", BC2), ("G2",), ("ATT", AB3),
)
KEYS = KV_HEADS * WIDTH
HALVES = ((0, WIDTH + KEYS), (WIDTH + KEYS, KEYS))
ST = 2 * STATE + 16

f32, bf16 = jnp.float32, jnp.bfloat16


def dot(a, b, ca, cb, precision=None):
    return lax.dot_general(
        a, b, (((ca,), (cb,)), ((), ())), precision=precision, preferred_element_type=f32
    )


def kernel(
    q_hbm, k_hbm, v_hbm, seg_ref, x_hbm, b_hbm, c_hbm, step_ref, rate_ref, skip_ref, g_hbm,
    ao_ref, mo_ref, dg_ref, q_ref, x_ref, b_ref, c_ref, g_ref, in_sem,
    kvb, qs, acc, mrow, lrow, bias, st_own, st_row, r_out, r_in, f_out, f_in,
    d_ref, dh_ref, fexp_ref, near_ref, grad_part, g_own, g_ctx, g_dp,
    kv_ss, kv_rs, a_ss, a_rs, r_ss, r_rs, f_ss, f_rs, gc_ss, gc_rs, gd_ss, gd_rs,
):
    count = q_ref.shape[0]
    me = lax.axis_index("ctx")
    z, x = me // COLS, me % COLS

    def dev(dz, dx):
        return {"ctx": ((z + dz) % ROWS) * COLS + (x + dx) % COLS}

    def come_in(*pairs, first):
        return [
            pltpu.make_async_copy(src, to, in_sem.at[first + i]) for i, (src, to) in enumerate(pairs)
        ]

    def await_all(copies):
        for copy in copies:
            copy.wait()

    kv_in = come_in(
        (k_hbm, kvb.at[OWN, :, pl.ds(WIDTH, KEYS)]),
        (v_hbm, kvb.at[OWN, :, pl.ds(WIDTH + KEYS, KEYS)]), first=0,
    )
    mixer_in = come_in((b_hbm, b_ref), (c_hbm, c_ref), (x_hbm, x_ref), (g_hbm, g_ref), first=2)
    query_in = come_in((q_hbm, q_ref), first=6)
    for copy in kv_in + mixer_in + query_in:
        copy.start()

    n_ctx, n_dp = lax.axis_size("ctx"), lax.axis_size("dp")
    row = lax.axis_index("dp")
    barrier = pltpu.get_barrier_semaphore()

    def greet(axis, place, size):
        def one(k, _):
            to = {axis: (place + k) % size}
            pl.semaphore_signal(barrier, inc=1, device_id=to, device_id_type=MESH)
            return 0

        lax.fori_loop(1, size, one, 0)

    greet("ctx", me, n_ctx)
    greet("dp", row, n_dp)

    segrow = seg_ref[...].astype(f32)
    rr = lax.broadcasted_iota(jnp.int32, (count, count), 0)
    cc = lax.broadcasted_iota(jnp.int32, (count, count), 1)
    eye = rr == cc
    segcol = jnp.sum(jnp.where(eye, segrow, 0.0), axis=1, keepdims=True)
    lane = lax.broadcasted_iota(jnp.int32, (count, WIDTH), 1).astype(f32)
    onehot = jnp.where(lane == segcol, 1.0, 0.0).astype(bf16)
    other = jnp.where((lane != segcol) & (lane < 8.0), FAR_BELOW, 0.0).astype(bf16)
    kvb[OWN, :, :WIDTH] = other

    pl.semaphore_wait(barrier, n_ctx + n_dp - 2)
    await_all(kv_in)

    def kv_copy(src, slot, half, dz, dx, way=0):
        lanes = pl.ds(*HALVES[half])
        return pltpu.make_async_remote_copy(
            src_ref=kvb.at[src, :, lanes], dst_ref=kvb.at[slot, :, lanes],
            send_sem=kv_ss.at[slot, half, way], recv_sem=kv_rs.at[slot, half],
            device_id=dev(dz, dx), device_id_type=MESH,
        )

    sent, here, ways = [], set(), {}

    def send(when, source, slot, half, dz, dx, where):
        way = ways.get((slot, half, where), 0)
        ways[slot, half, where] = way + 1
        copy = (source, slot, half, dz, dx, way)

        @pl.when(when)
        def _():
            kv_copy(*copy).start()

        sent.append((when, copy))

    def ensure(slot, half, columns):
        todo = [k for k in columns if (slot, half, k) not in here]
        here.update((slot, half, k) for k in todo)
        if todo:
            when = me >= BACK[slot]
            if len(todo) < COLS:
                when = when & functools.reduce(jnp.logical_or, [x == k for k in todo])

            @pl.when(when)
            def _():
                kv_copy(OWN, slot, half, 0, 1).wait_recv()

    def pass_block(slot, half, to, source, start, by_z=False):
        first = -(-(BACK[slot] - to) // COLS)
        if source != OWN:
            ensure(source, half, (start,))
        if by_z:
            send((x == start) & (z >= first - 1) & (z < ROWS - 1), source, slot, half, 1, 0, start)
        else:
            send((x == start) & (z >= first), source, slot, half, 0, (to - start) % COLS, start)

    def near_block(slot, half, to, route="D"):
        if route == "D":
            pass_block(slot, half, to, P1 if to < STEP[slot] else OWN, (to - STEP[slot]) % COLS)
        else:
            back = 1 if route == "F" else -1
            pass_block(slot, half, to, AB1 if route == "F" else AB3, (to - back) % COLS)

    def far_block(slot, half, to, route):
        if route == "x":
            pass_block(slot, half, to, P2 if to < STEP[slot] else P1, (to - STEP[slot]) % COLS)
        elif route == "z":
            pass_block(slot, half, to, BEFORE[slot], to, True)
        else:
            back = 1 if route == "F" else -1
            pass_block(slot, half, to, BC1 if route == "F" else BC3, (to - back) % COLS)

    def two_back(half, to, route):
        if route == "F":
            ensure(P1, half, range(COLS))
            send(z == to - 1, P1, P2, half, 1, 0, 0)
        elif route == "D":
            send(z == to - 2, OWN, P2, half, 2, 0, 0)
        else:
            send(z == to - 2, OWN, RELAY, half, -1, 0, 0)

    def relayed(half):
        @pl.when(z == ROWS - 1)
        def _():
            kv_copy(OWN, RELAY, half, 0, 1).wait_recv()

        send(z == ROWS - 1, RELAY, P2, half, -1, 0, 0)

    mask = (cc <= rr) & (segrow == segcol)
    upper = jnp.where(rr <= cc, 1.0, 0.0)
    eyef = jnp.where(eye, 1.0, 0.0)
    keep = jnp.where(segrow == segrow[:, count - 1 : count], 1.0, 0.0)
    live = jnp.where(segrow == segrow[:, 0:1], 1.0, 0.0)
    h16 = lax.broadcasted_iota(jnp.int32, (2 * PER, GW), 0) % PER
    spread = jnp.where(h16 == lax.broadcasted_iota(jnp.int32, (2 * PER, GW), 1) // HEAD_P, 1.0, 0.0)
    spread_bf = spread.astype(bf16)
    hi = lax.Precision.HIGHEST
    low_half = lax.broadcasted_iota(jnp.int32, (count, 2 * HEAD_P), 1) < HEAD_P
    meta_rows = lax.broadcasted_iota(jnp.int32, (16, GW), 0)
    last_own, first_own = segrow[:, count - 1 : count], segrow[:, 0:1]

    def expand(value):
        top = value.astype(bf16)
        rest = (value - top.astype(f32)).astype(bf16)
        return dot(jnp.concatenate([top, rest], axis=0), spread_bf, 0, 0)

    head_rows = lax.broadcasted_iota(jnp.int32, (PER, 1), 0)

    def per_head(ref, g):
        out = jnp.zeros((PER, 1), f32)
        for j in range(PER):
            out = jnp.where(head_rows == j, ref[g * PER + j], out)
        return out

    grad_part[...] = jnp.zeros_like(grad_part)

    def pack(span, last, first):
        top = span.astype(bf16).astype(f32)
        middle = (span - top).astype(bf16).astype(f32)
        out = jnp.where(meta_rows == 0, top, jnp.where(meta_rows == 1, middle, span - top - middle))
        out = jnp.where(meta_rows == 3, last, jnp.where(meta_rows == 4, first, out))
        return out.astype(bf16)

    def unpack(block):
        m = block.astype(f32)
        return m[0:1] + m[1:2] + m[2:3], m[3:4], m[4:5]

    def mixer_group(g, _):
        cols = pl.ds(pl.multiple_of(g * GW, GW), GW)
        ncols = pl.ds(pl.multiple_of(g * STATE, STATE), STATE)
        steps = step_ref[pl.ds(pl.multiple_of(g * PER, PER), PER), :]
        cs = dot(steps, upper, 1, 0, hi) * (-jnp.exp(per_head(rate_ref, g)))
        skip_row = jnp.sum(spread[:PER] * per_head(skip_ref, g), axis=0, keepdims=True)
        cst = dot(eyef, cs, 1, 1, hi)
        span = cs[:, count - 1 : count]
        tail = span - cs
        e = jnp.exp(tail) * keep
        f = jnp.exp(cs) * live
        xg, gg = x_ref[:, cols], g_ref[:, cols]
        bg, cg = b_ref[:, ncols].astype(bf16), c_ref[:, ncols].astype(bf16)
        right = jnp.concatenate([(xg * expand(e)).astype(bf16), (xg * expand(e * tail)).astype(bf16)], axis=1)
        sh = dot(bg, right, 0, 0).astype(bf16)
        st_own[g % 2, g // 2, :STATE] = sh[:, :GW]
        st_own[g % 2, g // 2, STATE : 2 * STATE] = sh[:, GW:]
        fe = expand(f)
        fexp_ref[g] = fe
        right = jnp.concatenate([(gg * fe).astype(bf16), (gg * expand(f * cs)).astype(bf16)], axis=1)
        dd = dot(cg, right, 0, 0)
        d_ref[g] = dd[:, :GW]
        dh_ref[g] = dd[:, GW:]
        span_row = jnp.sum(spread[:PER] * span, axis=0, keepdims=True)
        st_own[g % 2, g // 2, 2 * STATE :] = pack(span_row, last_own, first_own)
        inner = dot(cg, bg, 1, 1)
        sums = []
        for pair in range(PER // 2):
            lanes = slice(pair * 2 * HEAD_P, (pair + 1) * 2 * HEAD_P)
            xp, gp = xg[:, lanes], gg[:, lanes]
            xpb, gpb = xp.astype(bf16), gp.astype(bf16)
            near = None
            for half in range(2):
                j = pair * 2 + half
                mine = low_half if half == 0 else jnp.logical_not(low_half)
                gap = jnp.where(mask, cst[:, j : j + 1] - cs[j : j + 1, :], FAR_BELOW)
                weight = jnp.exp(gap) * inner
                pairs = dot(jnp.where(mine, gpb, jnp.zeros_like(gpb)), xpb, 1, 1)
                sums.append(jnp.sum(weight * gap * pairs, axis=0, keepdims=True))
                part = dot(weight.astype(bf16), jnp.where(mine, xpb, jnp.zeros_like(xpb)), 1, 0)
                near = part if near is None else near + part
            at = pl.ds(pl.multiple_of(g * GW + pair * 2 * HEAD_P, 2 * HEAD_P), 2 * HEAD_P)
            near_ref[:, at] = near + xp * skip_row[:, lanes]
        sums = jnp.concatenate(sums, axis=0)
        rest = jnp.concatenate([sums[:, WIDTH:], jnp.zeros((PER, 2 * WIDTH - count), f32)], axis=1)
        grad_part[pl.ds(pl.multiple_of(g * PER, PER), PER), :] = sums[:, :WIDTH] + rest
        return 0

    def a_copy(c, d):
        return pltpu.make_async_remote_copy(
            src_ref=st_own.at[c, (x + d) % COLS], dst_ref=st_row.at[c, x],
            send_sem=a_ss.at[c, d - 1], recv_sem=a_rs.at[c, d - 1],
            device_id=dev(0, d), device_id_type=MESH,
        )

    def mixer_half(c):
        if c == 0:
            await_all(mixer_in)
        lax.fori_loop(0, GROUPS // 2, lambda k, u: mixer_group(2 * k + c, u), 0)
        for d in (2, 1, 3):
            a_copy(c, d).start()
        st_row[c, x] = st_own[c, x]

    scale = math.log2(math.e) / math.sqrt(WIDTH)

    def scores(slot, h):
        at = pl.ds(pl.multiple_of((1 + h) * WIDTH, WIDTH), WIDTH)
        return dot(jnp.concatenate([kvb[slot, :, at], kvb[slot, :, :WIDTH]], axis=1), qs[h], 1, 1)

    def values_of(slot, h):
        return kvb[slot, :, pl.ds(pl.multiple_of((1 + KV_HEADS + h) * WIDTH, WIDTH), WIDTH)]

    def own_head(h, _):
        s = scores(OWN, h) + bias[...]
        top = jnp.max(s, axis=0, keepdims=True)
        w = jnp.exp2((s - top) * scale)
        mrow[pl.ds(h, 1), :] = top
        lrow[pl.ds(h, 1), :] = jnp.sum(w, axis=0, keepdims=True)
        acc[h] = dot(values_of(OWN, h), w.astype(bf16), 0, 0)
        return 0

    def attend_own():
        await_all(query_in)
        for h in range(KV_HEADS):
            for r in range(REP):
                head = h * REP + r
                qs[h, r * count : (r + 1) * count, :WIDTH] = q_ref[:, head * WIDTH : (head + 1) * WIDTH]
                qs[h, r * count : (r + 1) * count, WIDTH:] = onehot
        causal = jnp.where(rr <= cc, 0.0, FAR_BELOW)
        bias[...] = jnp.concatenate([causal] * REP, axis=1)
        lax.fori_loop(0, KV_HEADS, own_head, 0)

    def attend(slot):
        def head(h, _):
            s = scores(slot, h)
            before = mrow[pl.ds(h, 1), :]
            top = jnp.maximum(before, jnp.max(s, axis=0, keepdims=True))
            w = jnp.exp2((s - top) * scale)
            fade = jnp.exp2((before - top) * scale)
            mrow[pl.ds(h, 1), :] = top
            lrow[pl.ds(h, 1), :] = lrow[pl.ds(h, 1), :] * fade + jnp.sum(w, axis=0, keepdims=True)
            acc[h] = acc[h] * fade + dot(values_of(slot, h), w.astype(bf16), 0, 0)
            return 0

        lax.fori_loop(0, KV_HEADS, head, 0)

    def states(ref, *at):
        return ref[(*at, slice(0, STATE))].astype(f32), ref[(*at, slice(STATE, 2 * STATE))].astype(f32)

    def facts(ref, *at):
        return unpack(ref[(*at, slice(2 * STATE, ST))])

    def join(s, hat, last, ref, *at):
        span, after, _ = facts(ref, *at)
        s_b, hat_b = states(ref, *at)
        fade = jnp.where(last == after, jnp.exp(span), 0.0)
        return fade * s + s_b, fade * (hat + span * s) + hat_b, after

    def r_copy(c, dz):
        return pltpu.make_async_remote_copy(
            src_ref=r_out.at[c], dst_ref=r_in.at[c, dz - 1], send_sem=r_ss.at[c, dz - 1],
            recv_sem=r_rs.at[c, dz - 1], device_id=dev(dz, 0), device_id_type=MESH,
        )

    def row_total(c):
        for d in (2, 1, 3):
            a_copy(c, d).wait_recv()
        s, hat = states(st_row, c, 0)
        total, last, _ = facts(st_row, c, 0)
        for k in range(1, COLS):
            total = total + facts(st_row, c, k)[0]
            s, hat, last = join(s, hat, last, st_row, c, k)
        r_out[c, :STATE] = s.astype(bf16)
        r_out[c, STATE : 2 * STATE] = hat.astype(bf16)
        r_out[c, 2 * STATE :] = pack(total, last, last)
        for dz in (1, 2):
            @pl.when(z + dz < ROWS)
            def _(dz=dz):
                r_copy(c, dz).start()

            @pl.when(z - dz < 0)
            def _(dz=dz):
                r_in[c, dz - 1, : 2 * STATE] = jnp.zeros((2 * STATE, GW), bf16)
                r_in[c, dz - 1, 2 * STATE :] = jnp.full((16, GW), -1.0, bf16)

    def f_copy(c, d):
        return pltpu.make_async_remote_copy(
            src_ref=f_out.at[c, (x + d) % COLS], dst_ref=f_in.at[c, x],
            send_sem=f_ss.at[c, d - 1], recv_sem=f_rs.at[c, d - 1],
            device_id=dev(0, d), device_id_type=MESH,
        )

    def entering(c):
        for dz in (1, 2):
            @pl.when(z - dz >= 0)
            def _(dz=dz):
                r_copy(c, dz).wait_recv()
        s, hat = states(r_in, c, 1)
        s, hat, last = join(s, hat, facts(r_in, c, 1)[1], r_in, c, 0)
        for k in range(COLS):
            goes_on = jnp.where(facts(st_row, c, k)[2] == last, 1.0, 0.0)
            f_out[c, k, :STATE] = (s * goes_on).astype(bf16)
            f_out[c, k, STATE:] = (hat * goes_on).astype(bf16)
            if k < COLS - 1:
                s, hat, last = join(s, hat, last, st_row, c, k)
        for d in (2, 1, 3):
            f_copy(c, d).start()
        f_in[c, x] = f_out[c, x]

    def meet(slot):
        ensure(slot, 0, range(COLS))
        ensure(slot, 1, range(COLS))

        @pl.when(me >= BACK[slot])
        def _():
            attend(slot)

    def far_group(c, k):
        g = 2 * k + c
        cols = pl.ds(pl.multiple_of(g * GW, GW), GW)
        ncols = pl.ds(pl.multiple_of(g * STATE, STATE), STATE)
        s_in, hat_in = f_in[c, k, :STATE], f_in[c, k, STATE:]
        far = dot(c_ref[:, ncols].astype(bf16), s_in, 1, 0) * fexp_ref[g]
        mo_ref[:, cols] = (near_ref[:, cols] + far).astype(bf16)
        terms = hat_in.astype(f32) * d_ref[g] + s_in.astype(f32) * dh_ref[g]
        by_head = spread[:PER] * jnp.sum(terms, axis=0, keepdims=True)
        at = pl.ds(pl.multiple_of(g * PER, PER), PER)
        grad_part[at, :] = grad_part[at, :] + sum(by_head[:, i * WIDTH : (i + 1) * WIDTH] for i in range(GW // WIDTH))
        return 0

    def far_half(c):
        for d in (2, 1, 3):
            f_copy(c, d).wait_recv()
        lax.fori_loop(0, GROUPS // 2, lambda k, _: far_group(c, k), 0)

    def gc_copy(k):
        return pltpu.make_async_remote_copy(
            src_ref=g_own.at[0], dst_ref=g_ctx.at[me], send_sem=gc_ss.at[k],
            recv_sem=gc_rs.at[k], device_id={"ctx": (me + k) % n_ctx}, device_id_type=MESH,
        )

    def gd_copy(k):
        return pltpu.make_async_remote_copy(
            src_ref=g_own.at[1], dst_ref=g_dp.at[row], send_sem=gd_ss.at[k],
            recv_sem=gd_rs.at[k], device_id={"dp": (row + k) % n_dp}, device_id_type=MESH,
        )

    def each(first, last, act):
        def one(k, _):
            act(k)
            return 0

        lax.fori_loop(first, last, one, 0)

    def window_sum():
        g_own[0] = dot(jnp.ones((8, WIDTH), f32), grad_part[...], 1, 1, hi)
        g_ctx[me] = g_own[0]
        each(1, n_ctx, lambda k: gc_copy(k).start())

    def whole_sum():
        each(1, n_ctx, lambda k: gc_copy(k).wait_recv())
        g_own[1] = lax.fori_loop(0, n_ctx, lambda k, t: t + g_ctx[k], jnp.zeros((8, WIDTH), f32))
        g_dp[row] = g_own[1]
        each(1, n_dp, lambda k: gd_copy(k).start())

    for name, *what in PLAN:
        if name == "P1":
            send(z < ROWS - 1, OWN, P1, what[0], 1, 0, 0)
        elif name == "ATT" and what[0] == OWN:
            attend_own()
        elif name == "ATT":
            meet(what[0])
        else:
            {"P2": two_back, "RL": relayed, "AB": near_block, "BC": far_block,
             "AB2": lambda half, to, route: near_block(AB2, half, to, route), "MIX": mixer_half, "RT": row_total, "ENT": entering, "FAR": far_half,
             "G1": window_sum, "G2": whole_sum}[name](*what)

    for h in range(KV_HEADS):
        out = (acc[h] / lrow[h : h + 1, :]).T.astype(bf16)
        for r in range(REP):
            head = h * REP + r
            ao_ref[:, head * WIDTH : (head + 1) * WIDTH] = out[r * count : (r + 1) * count]

    each(1, n_dp, lambda k: gd_copy(k).wait_recv())
    total = lax.fori_loop(0, n_dp, lambda k, t: t + g_dp[k], jnp.zeros((8, WIDTH), f32))
    dg_ref[...] = total * (1.0 / (n_ctx * n_dp * count))
    each(1, n_ctx, lambda k: gc_copy(k).wait_send())
    each(1, n_dp, lambda k: gd_copy(k).wait_send())

    for when, copy in sent:
        @pl.when(when)
        def _(copy=copy):
            kv_copy(*copy).wait_send()

    for c in range(2):
        for d in (1, 2, 3):
            a_copy(c, d).wait_send()
            f_copy(c, d).wait_send()
        for dz in (1, 2):
            @pl.when(z + dz < ROWS)
            def _(c=c, dz=dz):
                r_copy(c, dz).wait_send()


def fused(q, k, v, seg, x, b, c, step, rate, skip, g):
    count = q.shape[0]
    vmem = pl.BlockSpec(memory_space=pltpu.VMEM)
    smem = pl.BlockSpec(memory_space=pltpu.SMEM)
    hbm = pl.BlockSpec(memory_space=pl.ANY)
    dma = pltpu.SemaphoreType.DMA
    n_ctx, n_dp = lax.axis_size("ctx"), lax.axis_size("dp")
    return pl.pallas_call(
        kernel,
        out_shape=(
            jax.ShapeDtypeStruct((count, Q_HEADS * WIDTH), bf16),
            jax.ShapeDtypeStruct((count, SSD_HEADS * HEAD_P), bf16),
            jax.ShapeDtypeStruct((8, WIDTH), f32),
        ),
        in_specs=[hbm] * 3 + [vmem] + [hbm] * 3 + [vmem] + [smem] * 2 + [hbm],
        out_specs=(vmem,) * 3,
        scratch_shapes=[
            pltpu.VMEM((count, Q_HEADS * WIDTH), bf16),
            pltpu.VMEM((count, SSD_HEADS * HEAD_P), f32),
            pltpu.VMEM((count, GROUPS * STATE), f32),
            pltpu.VMEM((count, GROUPS * STATE), f32),
            pltpu.VMEM((count, SSD_HEADS * HEAD_P), f32),
            dma((7,)),
            pltpu.VMEM((10, count, KVW), bf16),
            pltpu.VMEM((KV_HEADS, REP * count, 2 * WIDTH), bf16),
            pltpu.VMEM((KV_HEADS, WIDTH, REP * count), f32),
            pltpu.VMEM((KV_HEADS, REP * count), f32),
            pltpu.VMEM((KV_HEADS, REP * count), f32),
            pltpu.VMEM((count, REP * count), f32),
            pltpu.VMEM((2, COLS, ST, GW), bf16),
            pltpu.VMEM((2, COLS, ST, GW), bf16),
            pltpu.VMEM((2, ST, GW), bf16),
            pltpu.VMEM((2, 2, ST, GW), bf16),
            pltpu.VMEM((2, COLS, 2 * STATE, GW), bf16),
            pltpu.VMEM((2, COLS, 2 * STATE, GW), bf16),
            pltpu.VMEM((GROUPS, STATE, GW), f32),
            pltpu.VMEM((GROUPS, STATE, GW), f32),
            pltpu.VMEM((GROUPS, count, GW), f32),
            pltpu.VMEM((count, SSD_HEADS * HEAD_P), f32),
            pltpu.VMEM((WIDTH, WIDTH), f32),
            pltpu.VMEM((2, 8, WIDTH), f32),
            pltpu.VMEM((n_ctx, 8, WIDTH), f32),
            pltpu.VMEM((n_dp, 8, WIDTH), f32),
            dma((10, 2, 4)), dma((10, 2)),
            dma((2, 3)), dma((2, 3)), dma((2, 2)), dma((2, 2)), dma((2, 3)), dma((2, 3)),
            dma((n_ctx,)), dma((n_ctx,)), dma((n_dp,)), dma((n_dp,)),
        ],
        compiler_params=pltpu.CompilerParams(
            collective_id=0, has_side_effects=True, vmem_limit_bytes=60 * 2**20
        ),
        name="fused_mixer_attention",
    )(q, k, v, seg, x, b, c, step, rate, skip, g)


def on_device(
    queries, keys, values, segment_ids, ssd_input, b_matrix, c_matrix, step_size,
    decay_log, skip_gain, cotangent,
):
    attention, mixed, decay_grad = fused(
        queries[0], keys[0], values[0], segment_ids, ssd_input[0], b_matrix[0], c_matrix[0],
        step_size[0], decay_log, skip_gain, cotangent[0],
    )
    return attention[None], mixed[None], decay_grad[0, :SSD_HEADS]


def solution(mesh):
    tok = P("dp", "ctx", None)
    return jax.shard_map(
        on_device,
        mesh=mesh,
        in_specs=(tok, tok, tok, P("dp", "ctx"), tok, tok, tok, P("dp", None, "ctx"), P(), P(), tok),
        out_specs=(tok, tok, P()),
        check_vma=False,
    )
```

time: 208 us -> 132 us (0.63)
  blocking collectives: 84.7 us -> 0 us
  Pallas kernels: 113 us -> 126 us
  other arithmetic: 3.79 us -> 0 us
    psum x1 -> x0, blocking collectives: 84.7 us -> none  [on_device(): grand = lax.psum(part, ('dp', 'ctx'))]
    pallas_call x1, Pallas kernels: 113 us -> 126 us  [fused(): pl.pallas_call(kernel, out_shape=(jax.ShapeDtypeStruct((count, Q_HEADS *...]
where the time goes in v2:
time: 132 us
  Pallas kernels  126 us (95%)
  local copies, waits for them, and re-layouts  5.16 us (4%)
    pallas_call x1, Pallas kernels, fused(): pl.pallas_call(kernel, out_shape=(jax.ShapeDtypeStruct((count, Q_HEADS *...  126 us
    unnamed x4, local copies, waits for them, and re-layouts  3.97 us

profile of v2, /device:TPU:1, one launch (start us, length us, event | category | flops | bytes accessed | tf_op | source)
XLA Modules:
  0.0 131.9 jit_solution(7983092325591157245)
XLA Ops:
  0.6 126.1 %fused_mixer_attention.1 = (bf16[192,4096]{1,0:T(8,128)(2,1)}, bf16[192,4096]{1,0:T(8,128)(2,1)}, f32[8,128]{1,0:T(8,128)}) custom-call(bf16[192,4096]{1,0:T(8,128)(2,1)} %bitcast.16, bf16[192,1024]{1,0:T(8,128)(2,1)} %bitcast.19, bf16[192,1024]{1,0:T(8,128)(2,1)} %bitcast.20, s32[1,192]{1,0:T(1,128)} %seg_ref.1, f32[192,4096]{1,0:T(8,128)} %bitcast.12, ...), custom_call_target="tpu_custom_call" | custom-call | tf_op jit(solution)/shard_map/fused_mixer_attention/pallas_call | solution.py:506
  126.8 1.2 slice_bitcast_fusion
  128.0 0.0 copy-start
  128.0 2.8 %copy.16 = bf16[1,192,4096]{2,1,0:T(8,128)(2,1)} copy(bf16[1,192,4096]{2,1,0:T(8,128)(2,1)} %bitcast.15) | data formatting | bytes 3145728
  130.8 0.0 copy-done
  130.8 1.1 copy.17
Async XLA Ops:
  128.0 2.8 %copy-start = (bf16[192,4096]{1,0:T(8,128)(2,1)S(1)}, bf16[192,4096]{1,0:T(8,128)(2,1)}, u32[]{:S(2)}) copy-start(bf16[192,4096]{1,0:T(8,128)(2,1)} %get-tuple-element.7) | copy-start | bytes 4718596

commit v3 on v2

--- a/solution.py
+++ b/solution.py
@@ -30,24 +30,26 @@
 STEP = {AB1: 1, AB2: 2, AB3: 3, BC1: 1, BC2: 2, BC3: 3}
 BEFORE = {BC1: AB1, BC2: AB2, BC3: AB3}
 PLAN = (
-    ("P2", 1, 2, "R"), ("P1", 0), ("AB", AB1, 0, 1), ("AB", AB1, 1, 3), ("AB2", 0, 3, "D"), ("P1", 1),
-    ("AB", AB1, 1, 2), ("MIX", 0), ("MIX", 1), ("AB", AB1, 1, 1), ("BC", BC3, 0, 3, "x"),
-    ("P2", 1, 3, "D"), ("P2", 0, 2, "D"), ("BC", BC1, 0, 1, "z"), ("AB", AB1, 0, 0),
-    ("BC", BC1, 1, 2, "z"), ("AB", AB1, 0, 2), ("AB2", 0, 2, "F"), ("AB", AB1, 1, 0), ("AB2", 1, 0, "D"),
-    ("AB", AB3, 1, 1), ("ATT", OWN), ("AB", AB3, 1, 0), ("P2", 0, 3, "F"), ("AB", AB3, 1, 2),
-    ("AB", AB1, 0, 3), ("BC", BC3, 0, 2, "x"), ("BC", BC2, 0, 3, "z"), ("RT", 0), ("AB2", 1, 3, "D"),
-    ("RL", 1), ("BC", BC1, 1, 1, "z"), ("AB", AB3, 0, 1), ("BC", BC3, 0, 0, "x"), ("AB2", 1, 1, "M"),
-    ("ENT", 0), ("BC", BC3, 1, 2, "z"), ("BC", BC2, 1, 3, "F"), ("BC", BC1, 0, 2, "x"), ("AB", AB3, 0, 2),
-    ("BC", BC3, 1, 3, "x"), ("AB2", 1, 2, "F"), ("BC", BC1, 1, 3, "x"), ("BC", BC3, 1, 0, "z"),
-    ("ATT", P2), ("BC", BC3, 1, 1, "z"), ("AB2", 0, 1, "F"), ("BC", BC3, 0, 1, "x"), ("AB", AB3, 1, 3),
-    ("RT", 1), ("BC", BC1, 1, 0, "x"), ("BC", BC2, 0, 2, "z"), ("BC", BC1, 0, 0, "z"), ("ATT", P1),
-    ("ATT", AB1), ("AB2", 0, 0, "M"), ("BC", BC1, 0, 3, "z"), ("BC", BC2, 0, 1, "z"),
-    ("BC", BC2, 1, 0, "z"), ("FAR", 0), ("ENT", 1), ("BC", BC2, 0, 0, "z"), ("ATT", AB2),
-    ("BC", BC2, 1, 1, "z"), ("AB", AB3, 0, 0), ("BC", BC2, 1, 2, "z"), ("AB", AB3, 0, 3), ("ATT", BC3),
-    ("ATT", BC1), ("FAR", 1), ("G1",), ("ATT", BC2), ("G2",), ("ATT", AB3),
+    ("AB2", 1, 3, "D"), ("P1", 0), ("P2", 0, 2, "R"), ("P2", 1, 2, "R"), ("AB", AB1, 1, 2),
+    ("AB", AB1, 1, 1), ("AB", AB1, 1, 3), ("MIX", 0), ("P1", 1), ("MIX", 1), ("ATT", OWN, 0),
+    ("AB", AB3, 1, 0), ("ATT", P1, 0), ("RT", 0), ("AB2", 1, 1, "D"), ("P2", 1, 3, "D"), ("AB", AB3, 1, 3),
+    ("AB", AB3, 0, 2), ("AB", AB3, 0, 0), ("AB", AB3, 0, 3), ("AB", AB1, 0, 3), ("AB", AB1, 0, 0),
+    ("AB", AB1, 0, 1), ("AB", AB3, 0, 1), ("AB", AB1, 0, 2), ("RT", 1), ("BC", BC1, 0, 2, "z"), ("RL", 1),
+    ("AB2", 0, 1, "F"), ("AB2", 0, 2, "F"), ("BC", BC3, 0, 3, "x"), ("BC", BC1, 0, 1, "z"),
+    ("BC", BC1, 1, 3, "z"), ("P2", 0, 3, "D"), ("AB", AB1, 1, 0), ("AB2", 0, 3, "F"), ("ATT", OWN, 1),
+    ("AB2", 1, 0, "D"), ("AB", AB3, 1, 2), ("BC", BC1, 1, 0, "x"), ("BC", BC1, 0, 0, "z"), ("ATT", AB1, 0),
+    ("BC", BC1, 1, 2, "x"), ("BC", BC1, 0, 3, "z"), ("AB2", 0, 0, "M"), ("AB", AB3, 1, 1),
+    ("BC", BC3, 0, 1, "z"), ("AB2", 1, 2, "M"), ("RL", 0), ("ATT", AB3, 0), ("BC", BC3, 0, 2, "z"),
+    ("ATT", P1, 1), ("BC", BC3, 1, 3, "z"), ("ENT", 0), ("ATT", AB1, 1), ("BC", BC3, 1, 2, "z"),
+    ("ATT", AB3, 1), ("ENT", 1), ("BC", BC3, 0, 0, "z"), ("BC", BC3, 1, 1, "x"), ("BC", BC1, 1, 1, "z"),
+    ("ATT", P2, 0), ("ATT", AB2, 0), ("BC", BC2, 0, 1, "F"), ("BC", BC2, 1, 2, "z"),
+    ("BC", BC2, 1, 0, "z"), ("BC", BC3, 1, 0, "x"), ("ATT", AB2, 1), ("ATT", BC1, 0),
+    ("BC", BC2, 0, 2, "F"), ("BC", BC2, 1, 3, "F"), ("BC", BC2, 0, 3, "z"), ("BC", BC2, 1, 1, "z"),
+    ("BC", BC2, 0, 0, "z"), ("ATT", P2, 1), ("ATT", BC3, 0), ("ATT", BC1, 1), ("FAR", 0), ("FAR", 1),
+    ("G1",), ("ATT", BC3, 1), ("ATT", BC2, 1), ("G2",), ("ATT", BC2, 0),
 )
-KEYS = KV_HEADS * WIDTH
-HALVES = ((0, WIDTH + KEYS), (WIDTH + KEYS, KEYS))
+KEYS = KV_HEADS * WIDTH // 2
+HALVES = ((0, WIDTH + 2 * KEYS), (WIDTH + 2 * KEYS, 2 * KEYS))
 ST = 2 * STATE + 16
 
 f32, bf16 = jnp.float32, jnp.bfloat16
@@ -83,11 +85,13 @@
             copy.wait()
 
     kv_in = come_in(
-        (k_hbm, kvb.at[OWN, :, pl.ds(WIDTH, KEYS)]),
-        (v_hbm, kvb.at[OWN, :, pl.ds(WIDTH + KEYS, KEYS)]), first=0,
+        *(
+            (src.at[:, pl.ds(half * KEYS, KEYS)], kvb.at[OWN, :, pl.ds(WIDTH + (2 * half + i) * KEYS, KEYS)])
+            for half in (0, 1) for i, src in enumerate((k_hbm, v_hbm))
+        ), first=0,
     )
-    mixer_in = come_in((b_hbm, b_ref), (c_hbm, c_ref), (x_hbm, x_ref), (g_hbm, g_ref), first=2)
-    query_in = come_in((q_hbm, q_ref), first=6)
+    mixer_in = come_in((b_hbm, b_ref), (c_hbm, c_ref), (x_hbm, x_ref), (g_hbm, g_ref), first=4)
+    query_in = come_in((q_hbm, q_ref), first=8)
     for copy in kv_in + mixer_in + query_in:
         copy.start()
 
@@ -297,12 +301,16 @@
 
     scale = math.log2(math.e) / math.sqrt(WIDTH)
 
+    def lanes_of(h, which):
+        at = WIDTH + (2 * (h // (KV_HEADS // 2)) + which) * KEYS + (h % (KV_HEADS // 2)) * WIDTH
+        return pl.ds(pl.multiple_of(at, WIDTH), WIDTH)
+
     def scores(slot, h):
-        at = pl.ds(pl.multiple_of((1 + h) * WIDTH, WIDTH), WIDTH)
-        return dot(jnp.concatenate([kvb[slot, :, at], kvb[slot, :, :WIDTH]], axis=1), qs[h], 1, 1)
+        keys = kvb[slot, :, lanes_of(h, 0)]
+        return dot(jnp.concatenate([keys, kvb[slot, :, :WIDTH]], axis=1), qs[h], 1, 1)
 
     def values_of(slot, h):
-        return kvb[slot, :, pl.ds(pl.multiple_of((1 + KV_HEADS + h) * WIDTH, WIDTH), WIDTH)]
+        return kvb[slot, :, lanes_of(h, 1)]
 
     def own_head(h, _):
         s = scores(OWN, h) + bias[...]
@@ -313,18 +321,23 @@
         acc[h] = dot(values_of(OWN, h), w.astype(bf16), 0, 0)
         return 0
 
-    def attend_own():
-        await_all(query_in)
-        for h in range(KV_HEADS):
+    def heads_of(half):
+        return half * KV_HEADS // 2, (half + 1) * KV_HEADS // 2
+
+    causal = jnp.where(rr <= cc, 0.0, FAR_BELOW)
+    bias[...] = jnp.concatenate([causal] * REP, axis=1)
+
+    def attend_own(half):
+        if half == 0:
+            await_all(query_in)
+        for h in range(*heads_of(half)):
             for r in range(REP):
                 head = h * REP + r
                 qs[h, r * count : (r + 1) * count, :WIDTH] = q_ref[:, head * WIDTH : (head + 1) * WIDTH]
                 qs[h, r * count : (r + 1) * count, WIDTH:] = onehot
-        causal = jnp.where(rr <= cc, 0.0, FAR_BELOW)
-        bias[...] = jnp.concatenate([causal] * REP, axis=1)
-        lax.fori_loop(0, KV_HEADS, own_head, 0)
-
-    def attend(slot):
+        lax.fori_loop(*heads_of(half), own_head, 0)
+
+    def attend(slot, half):
         def head(h, _):
             s = scores(slot, h)
             before = mrow[pl.ds(h, 1), :]
@@ -336,7 +349,7 @@
             acc[h] = acc[h] * fade + dot(values_of(slot, h), w.astype(bf16), 0, 0)
             return 0
 
-        lax.fori_loop(0, KV_HEADS, head, 0)
+        lax.fori_loop(*heads_of(half), head, 0)
 
     def states(ref, *at):
         return ref[(*at, slice(0, STATE))].astype(f32), ref[(*at, slice(STATE, 2 * STATE))].astype(f32)
@@ -401,13 +414,14 @@
             f_copy(c, d).start()
         f_in[c, x] = f_out[c, x]
 
-    def meet(slot):
+    def meet(slot, half):
         ensure(slot, 0, range(COLS))
-        ensure(slot, 1, range(COLS))
+        if half == 1:
+            ensure(slot, 1, range(COLS))
 
         @pl.when(me >= BACK[slot])
         def _():
-            attend(slot)
+            attend(slot, half)
 
     def far_group(c, k):
         g = 2 * k + c
@@ -461,9 +475,9 @@
         if name == "P1":
             send(z < ROWS - 1, OWN, P1, what[0], 1, 0, 0)
         elif name == "ATT" and what[0] == OWN:
-            attend_own()
+            attend_own(what[1])
         elif name == "ATT":
-            meet(what[0])
+            meet(*what)
         else:
             {"P2": two_back, "RL": relayed, "AB": near_block, "BC": far_block,
              "AB2": lambda half, to, route: near_block(AB2, half, to, route), "MIX": mixer_half, "RT": row_total, "ENT": entering, "FAR": far_half,
@@ -518,7 +532,7 @@
             pltpu.VMEM((count, GROUPS * STATE), f32),
             pltpu.VMEM((count, GROUPS * STATE), f32),
             pltpu.VMEM((count, SSD_HEADS * HEAD_P), f32),
-            dma((7,)),
+            dma((9,)),
             pltpu.VMEM((10, count, KVW), bf16),
             pltpu.VMEM((KV_HEADS, REP * count, 2 * WIDTH), bf16),
             pltpu.VMEM((KV_HEADS, WIDTH, REP * count), f32),

time: 132 us -> 120 us (0.909)
  Pallas kernels: 126 us -> 114 us
    pallas_call x1, Pallas kernels: 126 us -> 114 us  [fused(): pl.pallas_call(kernel, out_shape=(jax.ShapeDtypeStruct((count, Q_HEADS *...]
where the time goes in v3:
time: 120 us
  Pallas kernels  114 us (95%)
  local copies, waits for them, and re-layouts  5.16 us (4%)
    pallas_call x1, Pallas kernels, fused(): pl.pallas_call(kernel, out_shape=(jax.ShapeDtypeStruct((count, Q_HEADS *...  114 us
    unnamed x4, local copies, waits for them, and re-layouts  3.97 us

profile of v3, /device:TPU:1, one launch (start us, length us, event | category | flops | bytes accessed | tf_op | source)
XLA Modules:
  0.0 119.8 jit_solution(14072814738667044059)
XLA Ops:
  0.6 114.0 %fused_mixer_attention.1 = (bf16[192,4096]{1,0:T(8,128)(2,1)}, bf16[192,4096]{1,0:T(8,128)(2,1)}, f32[8,128]{1,0:T(8,128)}) custom-call(bf16[192,4096]{1,0:T(8,128)(2,1)} %bitcast.16, bf16[192,1024]{1,0:T(8,128)(2,1)} %bitcast.19, bf16[192,1024]{1,0:T(8,128)(2,1)} %bitcast.20, s32[1,192]{1,0:T(1,128)} %seg_ref.1, f32[192,4096]{1,0:T(8,128)} %bitcast.12, ...), custom_call_target="tpu_custom_call" | custom-call | tf_op jit(solution)/shard_map/fused_mixer_attention/pallas_call | solution.py:520
  114.7 1.2 slice_bitcast_fusion
  115.9 0.0 copy-start
  115.9 2.8 %copy.16 = bf16[1,192,4096]{2,1,0:T(8,128)(2,1)} copy(bf16[1,192,4096]{2,1,0:T(8,128)(2,1)} %bitcast.15) | data formatting | bytes 3145728
  118.7 0.0 copy-done
  118.7 1.1 copy.17
Async XLA Ops:
  115.9 2.8 %copy-start = (bf16[192,4096]{1,0:T(8,128)(2,1)S(1)}, bf16[192,4096]{1,0:T(8,128)(2,1)}, u32[]{:S(2)}) copy-start(bf16[192,4096]{1,0:T(8,128)(2,1)} %get-tuple-element.7) | copy-start | bytes 4718596

commit v4 on v3

--- a/solution.py
+++ b/solution.py
@@ -30,27 +30,28 @@
 STEP = {AB1: 1, AB2: 2, AB3: 3, BC1: 1, BC2: 2, BC3: 3}
 BEFORE = {BC1: AB1, BC2: AB2, BC3: AB3}
 PLAN = (
-    ("AB2", 1, 3, "D"), ("P1", 0), ("P2", 0, 2, "R"), ("P2", 1, 2, "R"), ("AB", AB1, 1, 2),
-    ("AB", AB1, 1, 1), ("AB", AB1, 1, 3), ("MIX", 0), ("P1", 1), ("MIX", 1), ("ATT", OWN, 0),
-    ("AB", AB3, 1, 0), ("ATT", P1, 0), ("RT", 0), ("AB2", 1, 1, "D"), ("P2", 1, 3, "D"), ("AB", AB3, 1, 3),
-    ("AB", AB3, 0, 2), ("AB", AB3, 0, 0), ("AB", AB3, 0, 3), ("AB", AB1, 0, 3), ("AB", AB1, 0, 0),
-    ("AB", AB1, 0, 1), ("AB", AB3, 0, 1), ("AB", AB1, 0, 2), ("RT", 1), ("BC", BC1, 0, 2, "z"), ("RL", 1),
-    ("AB2", 0, 1, "F"), ("AB2", 0, 2, "F"), ("BC", BC3, 0, 3, "x"), ("BC", BC1, 0, 1, "z"),
-    ("BC", BC1, 1, 3, "z"), ("P2", 0, 3, "D"), ("AB", AB1, 1, 0), ("AB2", 0, 3, "F"), ("ATT", OWN, 1),
-    ("AB2", 1, 0, "D"), ("AB", AB3, 1, 2), ("BC", BC1, 1, 0, "x"), ("BC", BC1, 0, 0, "z"), ("ATT", AB1, 0),
-    ("BC", BC1, 1, 2, "x"), ("BC", BC1, 0, 3, "z"), ("AB2", 0, 0, "M"), ("AB", AB3, 1, 1),
-    ("BC", BC3, 0, 1, "z"), ("AB2", 1, 2, "M"), ("RL", 0), ("ATT", AB3, 0), ("BC", BC3, 0, 2, "z"),
-    ("ATT", P1, 1), ("BC", BC3, 1, 3, "z"), ("ENT", 0), ("ATT", AB1, 1), ("BC", BC3, 1, 2, "z"),
-    ("ATT", AB3, 1), ("ENT", 1), ("BC", BC3, 0, 0, "z"), ("BC", BC3, 1, 1, "x"), ("BC", BC1, 1, 1, "z"),
-    ("ATT", P2, 0), ("ATT", AB2, 0), ("BC", BC2, 0, 1, "F"), ("BC", BC2, 1, 2, "z"),
-    ("BC", BC2, 1, 0, "z"), ("BC", BC3, 1, 0, "x"), ("ATT", AB2, 1), ("ATT", BC1, 0),
-    ("BC", BC2, 0, 2, "F"), ("BC", BC2, 1, 3, "F"), ("BC", BC2, 0, 3, "z"), ("BC", BC2, 1, 1, "z"),
-    ("BC", BC2, 0, 0, "z"), ("ATT", P2, 1), ("ATT", BC3, 0), ("ATT", BC1, 1), ("FAR", 0), ("FAR", 1),
-    ("G1",), ("ATT", BC3, 1), ("ATT", BC2, 1), ("G2",), ("ATT", BC2, 0),
+    ("P2", 0, 3, "D"), ("AB", AB1, 1, 2), ("AB", AB1, 0, 1), ("AB2", 0, 3, "D"), ("P1", 1),
+    ("AB", AB1, 0, 3), ("P1", 0), ("MIX", 0), ("P2", 1, 3, "D"), ("MIX", 1), ("P2", 1, 2, "F"),
+    ("ATT", OWN, 0), ("P2", 0, 2, "R"), ("AB", AB1, 0, 0), ("BC", BC1, 0, 1, "z"), ("ATT", P1, 0),
+    ("BC", BC1, 1, 2, "z"), ("AB", AB3, 0, 3), ("BC", BC1, 0, 3, "z"), ("AB", AB3, 1, 0),
+    ("AB", AB1, 0, 2), ("ATT", OWN, 1), ("AB", AB3, 1, 3), ("AB", AB1, 1, 1), ("AB", AB3, 0, 2),
+    ("AB", AB3, 0, 1), ("AB", AB3, 0, 0), ("AB", AB3, 1, 2), ("AB2", 1, 3, "F"), ("AB", AB1, 1, 3),
+    ("RT", 0), ("RL", 0), ("AB2", 0, 2, "F"), ("RT", 1), ("AB2", 0, 0, "M"), ("AB", AB1, 1, 0),
+    ("BC", BC1, 1, 1, "x"), ("BC", BC1, 1, 3, "x"), ("AB", AB3, 1, 1), ("ATT", P1, 1), ("ATT", P2, 1),
+    ("AB2", 1, 1, "M"), ("BC", BC3, 0, 2, "x"), ("BC", BC3, 0, 3, "x"), ("AB2", 1, 2, "F"),
+    ("BC", BC1, 0, 0, "z"), ("AB2", 0, 1, "F"), ("BC", BC1, 1, 0, "x"), ("ATT", AB3, 1),
+    ("BC", BC3, 1, 3, "z"), ("BC", BC2, 1, 3, "z"), ("ENT", 0), ("ATT", AB1, 0), ("BC", BC3, 0, 0, "z"),
+    ("BC", BC1, 0, 2, "z"), ("BC", BC3, 0, 1, "z"), ("ATT", AB3, 0), ("ATT", AB1, 1),
+    ("BC", BC3, 1, 1, "z"), ("ENT", 1), ("BC", BC3, 1, 0, "z"), ("ATT", BC1, 1), ("BC", BC2, 0, 1, "M"),
+    ("BC", BC3, 1, 2, "z"), ("AB2", 1, 0, "M"), ("ATT", BC1, 0), ("ATT", AB2, 0), ("ATT", P2, 0),
+    ("BC", BC2, 1, 1, "F"), ("BC", BC2, 0, 3, "z"), ("FAR", 0), ("BC", BC2, 1, 0, "x"),
+    ("BC", BC2, 1, 2, "F"), ("BC", BC2, 0, 2, "z"), ("BC", BC2, 0, 0, "z"), ("ATT", BC3, 0),
+    ("ATT", BC3, 1), ("FAR", 1), ("G1",), ("ATT", AB2, 1), ("G2",), ("ATT", BC2, 0), ("ATT", BC2, 1),
 )
 KEYS = KV_HEADS * WIDTH // 2
 HALVES = ((0, WIDTH + 2 * KEYS), (WIDTH + 2 * KEYS, 2 * KEYS))
 ST = 2 * STATE + 16
+PIECES = 6
 
 f32, bf16 = jnp.float32, jnp.bfloat16
 
@@ -63,7 +64,7 @@
 
 def kernel(
     q_hbm, k_hbm, v_hbm, seg_ref, x_hbm, b_hbm, c_hbm, step_ref, rate_ref, skip_ref, g_hbm,
-    ao_ref, mo_ref, dg_ref, q_ref, x_ref, b_ref, c_ref, g_ref, in_sem,
+    ao_hbm, mo_hbm, dg_ref, ao_ref, mo_ref, q_ref, x_ref, b_ref, c_ref, g_ref, in_sem, out_sem,
     kvb, qs, acc, mrow, lrow, bias, st_own, st_row, r_out, r_in, f_out, f_in,
     d_ref, dh_ref, fexp_ref, near_ref, grad_part, g_own, g_ctx, g_dp,
     kv_ss, kv_rs, a_ss, a_rs, r_ss, r_rs, f_ss, f_rs, gc_ss, gc_rs, gd_ss, gd_rs,
@@ -471,7 +472,22 @@
         g_dp[row] = g_own[1]
         each(1, n_dp, lambda k: gd_copy(k).start())
 
-    for name, *what in PLAN:
+    def attention_out(half):
+        lanes = pl.ds(half * REP * KEYS, REP * KEYS)
+        return pltpu.make_async_copy(ao_ref.at[:, lanes], ao_hbm.at[:, lanes], out_sem.at[half])
+
+    mixer_out = pltpu.make_async_copy(mo_ref, mo_hbm, out_sem.at[2])
+
+    def finish(half):
+        for h in range(*heads_of(half)):
+            out = (acc[h] / lrow[h : h + 1, :]).T.astype(bf16)
+            for r in range(REP):
+                head = h * REP + r
+                ao_ref[:, head * WIDTH : (head + 1) * WIDTH] = out[r * count : (r + 1) * count]
+        attention_out(half).start()
+
+    last = {step[0] + str(step[-1]) if step[0] == "ATT" else step[0]: i for i, step in enumerate(PLAN)}
+    for i, (name, *what) in enumerate(PLAN):
         if name == "P1":
             send(z < ROWS - 1, OWN, P1, what[0], 1, 0, 0)
         elif name == "ATT" and what[0] == OWN:
@@ -482,18 +498,18 @@
             {"P2": two_back, "RL": relayed, "AB": near_block, "BC": far_block,
              "AB2": lambda half, to, route: near_block(AB2, half, to, route), "MIX": mixer_half, "RT": row_total, "ENT": entering, "FAR": far_half,
              "G1": window_sum, "G2": whole_sum}[name](*what)
-
-    for h in range(KV_HEADS):
-        out = (acc[h] / lrow[h : h + 1, :]).T.astype(bf16)
-        for r in range(REP):
-            head = h * REP + r
-            ao_ref[:, head * WIDTH : (head + 1) * WIDTH] = out[r * count : (r + 1) * count]
+        if name == "ATT" and last["ATT" + str(what[1])] == i:
+            finish(what[1])
+        if name == "FAR" and last["FAR"] == i:
+            mixer_out.start()
 
     each(1, n_dp, lambda k: gd_copy(k).wait_recv())
     total = lax.fori_loop(0, n_dp, lambda k, t: t + g_dp[k], jnp.zeros((8, WIDTH), f32))
     dg_ref[...] = total * (1.0 / (n_ctx * n_dp * count))
     each(1, n_ctx, lambda k: gc_copy(k).wait_send())
     each(1, n_dp, lambda k: gd_copy(k).wait_send())
+
+    await_all([mixer_out, attention_out(0), attention_out(1)])
 
     for when, copy in sent:
         @pl.when(when)
@@ -525,14 +541,17 @@
             jax.ShapeDtypeStruct((8, WIDTH), f32),
         ),
         in_specs=[hbm] * 3 + [vmem] + [hbm] * 3 + [vmem] + [smem] * 2 + [hbm],
-        out_specs=(vmem,) * 3,
+        out_specs=(hbm, hbm, vmem),
         scratch_shapes=[
+            pltpu.VMEM((count, Q_HEADS * WIDTH), bf16),
+            pltpu.VMEM((count, SSD_HEADS * HEAD_P), bf16),
             pltpu.VMEM((count, Q_HEADS * WIDTH), bf16),
             pltpu.VMEM((count, SSD_HEADS * HEAD_P), f32),
             pltpu.VMEM((count, GROUPS * STATE), f32),
             pltpu.VMEM((count, GROUPS * STATE), f32),
             pltpu.VMEM((count, SSD_HEADS * HEAD_P), f32),
             dma((9,)),
+            dma((3,)),
             pltpu.VMEM((10, count, KVW), bf16),
             pltpu.VMEM((KV_HEADS, REP * count, 2 * WIDTH), bf16),
             pltpu.VMEM((KV_HEADS, WIDTH, REP * count), f32),
@@ -564,6 +583,47 @@
     )(q, k, v, seg, x, b, c, step, rate, skip, g)
 
 
+def hand_over_kernel(a_in, m_in, g_in, a_out, m_out, g_out, held, in_sem, out_sem):
+    rows = a_in.shape[0] // PIECES
+    pieces = [(j, i, pl.ds(i * rows, rows)) for i in range(PIECES) for j in range(2)]
+    come = [
+        pltpu.make_async_copy((a_in, m_in)[j].at[at], held.at[j, at], in_sem.at[j, i])
+        for j, i, at in pieces
+    ]
+    leave = [
+        pltpu.make_async_copy(held.at[j, at], (a_out, m_out)[j].at[at], out_sem.at[j, i])
+        for j, i, at in pieces
+    ]
+    for copy in come:
+        copy.start()
+    g_out[...] = g_in[0, :SSD_HEADS]
+    for copy, following in zip(come, leave):
+        copy.wait()
+        following.start()
+    for copy in leave:
+        copy.wait()
+
+
+def hand_over(a, m, g):
+    hbm, vmem = pl.BlockSpec(memory_space=pl.ANY), pl.BlockSpec(memory_space=pltpu.VMEM)
+    return pl.pallas_call(
+        hand_over_kernel,
+        out_shape=(
+            jax.ShapeDtypeStruct(a.shape, a.dtype),
+            jax.ShapeDtypeStruct(m.shape, m.dtype),
+            jax.ShapeDtypeStruct((SSD_HEADS,), f32),
+        ),
+        in_specs=[hbm, hbm, vmem],
+        out_specs=(hbm, hbm, vmem),
+        scratch_shapes=[
+            pltpu.VMEM((2, *a.shape), a.dtype),
+            pltpu.SemaphoreType.DMA((2, PIECES)),
+            pltpu.SemaphoreType.DMA((2, PIECES)),
+        ],
+        name="hand_over",
+    )(a, m, g)
+
+
 def on_device(
     queries, keys, values, segment_ids, ssd_input, b_matrix, c_matrix, step_size,
     decay_log, skip_gain, cotangent,
@@ -572,7 +632,8 @@
         queries[0], keys[0], values[0], segment_ids, ssd_input[0], b_matrix[0], c_matrix[0],
         step_size[0], decay_log, skip_gain, cotangent[0],
     )
-    return attention[None], mixed[None], decay_grad[0, :SSD_HEADS]
+    attention, mixed, decay_grad = hand_over(attention, mixed, decay_grad)
+    return attention[None], mixed[None], decay_grad
 
 
 def solution(mesh):

time: 120 us -> 118 us (0.983)
  local copies, waits for them, and re-layouts: 5.16 us -> 0 us
  Pallas kernels: 114 us -> 117 us
    pallas_call x0 -> x1, Pallas kernels: none -> 4 us  [hand_over(): pl.pallas_call(hand_over_kernel, out_shape=(jax.ShapeDtypeStruct(a.shape,...]
    unnamed x4 -> x0, local copies, waits for them, and re-layouts: 3.97 us -> none
    pallas_call x1, Pallas kernels: 114 us -> 113 us  [fused(): pl.pallas_call(kernel, out_shape=(jax.ShapeDtypeStruct((count, Q_HEADS *...]
where the time goes in v4:
time: 118 us; the launch traced here: 117 us
  Pallas kernels  117 us (99%)
    pallas_call x1, Pallas kernels, fused(): pl.pallas_call(kernel, out_shape=(jax.ShapeDtypeStruct((count, Q_HEADS *...  113 us
    pallas_call x1, Pallas kernels, hand_over(): pl.pallas_call(hand_over_kernel, out_shape=(jax.ShapeDtypeStruct(a.shape,...  4 us

profile of v4, /device:TPU:1, one launch (start us, length us, event | category | flops | bytes accessed | tf_op | source)
XLA Modules:
  0.0 117.5 jit_solution(2585031619355730969)
XLA Ops:
  0.6 112.7 %fused_mixer_attention.1 = (bf16[192,4096]{1,0:T(8,128)(2,1)}, bf16[192,4096]{1,0:T(8,128)(2,1)}, f32[8,128]{1,0:T(8,128)}) custom-call(bf16[192,4096]{1,0:T(8,128)(2,1)} %bitcast.12, bf16[192,1024]{1,0:T(8,128)(2,1)} %bitcast.15, bf16[192,1024]{1,0:T(8,128)(2,1)} %bitcast.16, s32[1,192]{1,0:T(1,128)} %seg_ref.1, f32[192,4096]{1,0:T(8,128)} %bitcast.10, ...), custom_call_target="tpu_custom_call" | custom-call | tf_op jit(solution)/shard_map/fused_mixer_attention/pallas_call | solution.py:536
  113.3 4.0 %hand_over.1 = (bf16[192,4096]{1,0:T(8,128)(2,1)}, bf16[192,4096]{1,0:T(8,128)(2,1)}, f32[64]{0:T(128)}) custom-call(bf16[192,4096]{1,0:T(8,128)(2,1)} %get-tuple-element.9.a_in, bf16[192,4096]{1,0:T(8,128)(2,1)} %get-tuple-element.10.m_in, f32[8,128]{1,0:T(8,128)} %get-tuple-element.11.g_in), custom_call_target="tpu_custom_call" | custom-call | tf_op jit(solution)/shard_map/hand_over/pallas_call | solution.py:609

commit v5 on v4

--- a/solution.py
+++ b/solution.py
@@ -336,7 +336,7 @@
                 head = h * REP + r
                 qs[h, r * count : (r + 1) * count, :WIDTH] = q_ref[:, head * WIDTH : (head + 1) * WIDTH]
                 qs[h, r * count : (r + 1) * count, WIDTH:] = onehot
-        lax.fori_loop(*heads_of(half), own_head, 0)
+        lax.fori_loop(*heads_of(half), own_head, 0, unroll=2)
 
     def attend(slot, half):
         def head(h, _):
@@ -350,7 +350,7 @@
             acc[h] = acc[h] * fade + dot(values_of(slot, h), w.astype(bf16), 0, 0)
             return 0
 
-        lax.fori_loop(*heads_of(half), head, 0)
+        lax.fori_loop(*heads_of(half), head, 0, unroll=2)
 
     def states(ref, *at):
         return ref[(*at, slice(0, STATE))].astype(f32), ref[(*at, slice(STATE, 2 * STATE))].astype(f32)

time: 118 us -> 117 us (level)
  no operation moved by 1% of the time
where the time goes in v5:
time: 117 us
  Pallas kernels  116 us (99%)
    pallas_call x1, Pallas kernels, fused(): pl.pallas_call(kernel, out_shape=(jax.ShapeDtypeStruct((count, Q_HEADS *...  112 us
    pallas_call x1, Pallas kernels, hand_over(): pl.pallas_call(hand_over_kernel, out_shape=(jax.ShapeDtypeStruct(a.shape,...  4 us

profile of v5, /device:TPU:1, one launch (start us, length us, event | category | flops | bytes accessed | tf_op | source)
XLA Modules:
  0.0 117.1 jit_solution(14013530207180907986)
XLA Ops:
  0.6 112.3 %fused_mixer_attention.1 = (bf16[192,4096]{1,0:T(8,128)(2,1)}, bf16[192,4096]{1,0:T(8,128)(2,1)}, f32[8,128]{1,0:T(8,128)}) custom-call(bf16[192,4096]{1,0:T(8,128)(2,1)} %bitcast.12, bf16[192,1024]{1,0:T(8,128)(2,1)} %bitcast.15, bf16[192,1024]{1,0:T(8,128)(2,1)} %bitcast.16, s32[1,192]{1,0:T(1,128)} %seg_ref.1, f32[192,4096]{1,0:T(8,128)} %bitcast.10, ...), custom_call_target="tpu_custom_call" | custom-call | tf_op jit(solution)/shard_map/fused_mixer_attention/pallas_call | solution.py:536
  112.9 4.0 %hand_over.1 = (bf16[192,4096]{1,0:T(8,128)(2,1)}, bf16[192,4096]{1,0:T(8,128)(2,1)}, f32[64]{0:T(128)}) custom-call(bf16[192,4096]{1,0:T(8,128)(2,1)} %get-tuple-element.9.a_in, bf16[192,4096]{1,0:T(8,128)(2,1)} %get-tuple-element.10.m_in, f32[8,128]{1,0:T(8,128)} %get-tuple-element.11.g_in), custom_call_target="tpu_custom_call" | custom-call | tf_op jit(solution)/shard_map/hand_over/pallas_call | solution.py:609
